TPU v7x, 768 devices: a whole 4x8x12 slice. The times are simulated.
768 devices in a mesh: row: 64 (over x, y, core), col: 12 (over z).
Axes of the slice: x: 4, y: 8, z: 12, core: 2. Of those that a mesh axis runs over, the one named last changes fastest.
Arguments:
- x_feat: bfloat16 [786432, 128], P(('row', 'col')), may hold values from -6 to 6
- weight: bfloat16 [128, 256], replicated, may hold values from -0.5 to 0.5
- tile_values: bfloat16 [61440, 128, 128], P(('row', 'col')), may hold values from 0 to 0.024169922
- tile_dst: int32 [61440], P(('row', 'col')), may hold values from 0 to 63
- tile_slot: int32 [61440], P(('row', 'col')), may hold values from 0 to 23, as said below
- src_blocks: int32 [9216, 2], P(('row', 'col')), may hold values from 0 to 7, as said below
- tile_count: int32 [768], P(('row', 'col')), may hold values from 10 to 80, as said below
- cotangent: bfloat16 [98304, 256], P(('row', 'col')), may hold values from -0.046875 to 0.046875
Outputs:
- layer_out: bfloat16 [98304, 256], P(('row', 'col'))
- weight_grad: float32 [128, 256], replicated
Inputs may be any that keep to these rules, and one draw needn't show every extreme that they name: `tile_slot`: A tile names one of the 12 * 2 listed source blocks of its device. `src_blocks`: each row lists 2 distinct source blocks of one col peer. `tile_count`: some device has all 80 slots live.
All inputs are finite; a program needn't handle non-finite values.
Results may differ from a plain program's by a relative error of at most 0.0053.
Values may be sent and summed in bfloat16 or wider, within the bound.
No kernel may reach another device: no remote copies, remote signals or barrier semaphores. Data moves between devices by JAX's collectives and lax.ppermute only.
A program may use at most 32 MiB of HBM per device.

v0:
```python
import jax
import jax.numpy as jnp
from jax import lax
from jax.sharding import PartitionSpec as P


def body(x_feat, weight, tile_values, tile_dst, tile_slot, src_blocks, tile_count, cotangent):
    block = tile_values.shape[1]
    d_in = x_feat.shape[1]
    columns = lax.axis_size("col")
    rows_axis = lax.axis_size("row")
    held = x_feat.shape[0] // block
    listed = src_blocks.shape[1]
    slots_total = tile_values.shape[0]
    dst_own = cotangent.shape[0] // block
    dst_total = rows_axis * dst_own
    whole = lax.all_gather(x_feat, "col", axis=0, tiled=True)
    pool = whole.reshape(columns * held, block, d_in)
    peer = tile_slot // listed
    where = peer * held + src_blocks[peer, tile_slot % listed]
    count = tile_count[0]
    live = (jnp.arange(slots_total, dtype=jnp.int32) < count).astype(jnp.float32)
    product = jnp.einsum(
        "tij,tjf->tif", tile_values, pool[where], preferred_element_type=jnp.float32
    )
    targets = jnp.arange(dst_total, dtype=jnp.int32)
    onehot = (tile_dst[:, None] == targets[None, :]).astype(jnp.float32) * live[:, None]
    partial_sum = jnp.einsum("tb,tif->bif", onehot, product, precision=lax.Precision.HIGHEST)
    reduced = lax.psum_scatter(
        partial_sum.reshape(dst_total * block, d_in), "row", scatter_dimension=0, tiled=True
    )
    aggregated = reduced.astype(jnp.bfloat16)
    pre = jnp.dot(aggregated, weight, preferred_element_type=jnp.float32)
    sig = jax.nn.sigmoid(pre)
    layer_out = (pre * sig).astype(jnp.bfloat16)
    grad_pre = (cotangent.astype(jnp.float32) * sig * (1.0 + pre * (1.0 - sig))).astype(
        jnp.bfloat16
    )
    local_grad = lax.dot_general(
        aggregated, grad_pre, (((0,), (0,)), ((), ())), preferred_element_type=jnp.float32
    )
    weight_grad = lax.psum(local_grad, ("row", "col"))
    return (layer_out, weight_grad)


def solution(mesh):
    return jax.shard_map(
        body,
        mesh=mesh,
        in_specs=(
            P(("row", "col"), None),
            P(),
            P(("row", "col"), None, None),
            P(("row", "col")),
            P(("row", "col")),
            P(("row", "col"), None),
            P(("row", "col")),
            P(("row", "col"), None),
        ),
        out_specs=(P(("row", "col"), None), P()),
        check_vma=False,
    )
```

profile of v0, /device:TPU:1, one launch (start us, length us, event | category | flops | bytes accessed | tf_op | source)
XLA Modules:
  0.0 737.0 jit_solution(3882650579272013109)
XLA Ops:
  7.2 0.0 copy-start
  7.2 0.0 all-gather.2.cloned.1.call-start
  7.2 0.7 all-gather.2.cloned.1.call-update
  7.9 0.0 reduce-scatter.2.cloned.1.call-start
  8.6 0.7 fusion.13
  9.3 2.2 gather_fusion
  11.5 64.7 %all-gather.2.cloned.1.call-done = bf16[12288,128]{1,0:T(8,128)(2,1)} async-done(((bf16[1024,128]{1,0:T(8,128)(2,1)}), bf16[12288,128]{1,0:T(8,128)(2,1)}) %all-gather.2.cloned.1.call-update) | async-done | bytes 3145744 | tf_op jit(solution)/shard_map/all_gather | solution.py:17
  76.2 4.4 gather_fusion.1
  80.6 0.0 copy-done
  80.6 6.0 fusion.18
  86.6 0.0 copy-start.1
  86.6 6.4 copy.11
  93.0 0.0 copy-done.1
  93.0 5.8 fusion
  98.8 4.4 copy.10
  103.2 0.0 copy-start.2
  103.2 0.0 copy-start.3
  103.2 0.0 reduce-scatter.2.cloned.1.call-update
  103.2 0.0 all-reduce.2.cloned.1.call-start
  103.3 158.6 %reduce-scatter.2.cloned.1.call-done = f32[128,128]{1,0:T(8,128)} async-done(((f32[8192,128]{1,0:T(8,128)}), f32[128,128]{1,0:T(8,128)}) %reduce-scatter.2.cloned.1.call-update) | async-done | bytes 65552 | tf_op jit(solution)/shard_map/reduce_scatter | solution.py:29
  261.9 0.0 copy-done.2
  261.9 1.6 multiply_convert_fusion.1
  263.6 0.0 copy-done.3
  263.6 1.7 fusion.2
  265.2 0.0 all-reduce.2.cloned.1.call-update
  265.3 463.6 %all-reduce.2.cloned.1.call-done = f32[128,256]{1,0:T(8,128)} async-done(((f32[128,256]{1,0:T(8,128)}), f32[128,256]{1,0:T(8,128)}) %all-reduce.2.cloned.1.call-update) | async-done | bytes 131088 | tf_op jit(solution)/shard_map/psum | solution.py:42
  728.9 1.6 copy.14
  (3 shorter events, 0.0 us)
Async XLA Ops:
  7.2 73.4 %copy-start = (bf16[80,128,128]{2,1,0:T(8,128)(2,1)S(1)}, bf16[80,128,128]{2,1,0:T(8,128)(2,1)}, u32[]{:S(2)}) copy-start(bf16[80,128,128]{2,1,0:T(8,128)(2,1)} %param.10) | copy-start | bytes 7864324
  7.2 69.0 %all-gather.2.cloned.1.call-start = ((), (), s32[]{:S(2)}) async-start(), calls=%async_computation.1 | async-start | bytes 3407872 | tf_op jit(solution)/shard_map/all_gather | solution.py:17
  7.9 254.0 %reduce-scatter.2.cloned.1.call-start = ((), (), s32[]{:S(2)}) async-start(), calls=%async_computation.2 | async-start | bytes 4259840 | tf_op jit(solution)/shard_map/reduce_scatter | solution.py:29
  86.6 6.4 copy-start.1
  103.2 158.7 %copy-start.2 = (bf16[128,256]{1,0:T(8,128)(2,1)S(1)}, bf16[128,256]{1,0:T(8,128)(2,1)}, u32[]{:S(2)}) copy-start(bf16[128,256]{1,0:T(8,128)(2,1)} %param.9) | copy-start | bytes 196612
  103.2 160.3 %copy-start.3 = (bf16[128,256]{1,0:T(8,128)(2,1)S(1)}, bf16[128,256]{1,0:T(8,128)(2,1)}, u32[]{:S(2)}) copy-start(bf16[128,256]{1,0:T(8,128)(2,1)} %param.15) | copy-start | bytes 196612
  103.2 625.7 %all-reduce.2.cloned.1.call-start = ((), (), s32[]{:S(2)}) async-start(), calls=%async_computation.3 | async-start | bytes 262144 | tf_op jit(solution)/shard_map/psum | solution.py:42
Sparse Core Ops, SparseCore 0:
  10.4 65.7 all-gather.1
  103.3 158.5 reduce-scatter.1
  268.8 460.0 all-reduce.1
where the time goes:
time: 738 us; the launch traced here: 737 us
  waiting for transfers between devices  688 us (93%)
  local copies, waits for them, and re-layouts  19 us (3%)
  matrix products  15.2 us (2%)
  between operations  14.5 us (2%)
    psum x1, waiting for transfers between devices, body(): weight_grad = lax.psum(local_grad, ('row', 'col'))  464 us
    reduce_scatter x1, waiting for transfers between devices, body(): lax.psum_scatter(partial_sum.reshape(dst_total * block, d_in), 'row', sca...  159 us
    all_gather x1, waiting for transfers between devices, body(): whole = lax.all_gather(x_feat, 'col', axis=0, tiled=True)  64.7 us
  transfers between devices with their start and end apart: 3, of which 3 were waited for; matrix products, arithmetic and copies ran while one was open for 0% of the time, Pallas kernels for 0%

commit v1 on v0

v1 whole, which is shorter than its diff:
```python
import jax
import jax.numpy as jnp
from jax import lax
from jax.experimental import pallas as pl
from jax.experimental.pallas import tpu as pltpu
from jax.sharding import Mesh, PartitionSpec as P

BLK = 128
UNROLL = 8
AXES = ("x", "y", "core", "col")
ROW = ("x", "y", "core")
SIZES = (4, 8, 2, 12)

VMEM = pl.BlockSpec(memory_space=pltpu.VMEM)
SMEM = pl.BlockSpec(memory_space=pltpu.SMEM)
BF16 = jnp.bfloat16
F32 = jnp.float32


def pick_kernel(asked, x_ref, out_ref):
    peers, listed = out_ref.shape[0], out_ref.shape[1]
    for p in range(peers):
        for k in range(listed):
            out_ref[p, k] = x_ref[asked[p, 0, k]]


def pick(asked, x_feat):
    peers, listed = SIZES[3], 2
    return pl.pallas_call(
        pick_kernel,
        out_shape=jax.ShapeDtypeStruct((peers, listed, BLK, x_feat.shape[1]), BF16),
        in_specs=[SMEM, VMEM],
        out_specs=VMEM,
        name="pick_blocks",
    )(asked, x_feat.reshape(-1, BLK, x_feat.shape[1]))


def aggregate_kernel(dst, slot, count, core, tiles, sources, mine, theirs, acc):
    half = mine.shape[0]
    live = count[0]
    me = core[0]
    acc[...] = jnp.zeros_like(acc)

    def group(g, carry):
        for u in range(UNROLL):
            t = g * UNROLL + u
            d = dst[t]
            place = ((d & 1) ^ me) * half + (d >> 1)
            place = jnp.where(t < live, place, 2 * half)
            acc[place] += jnp.dot(tiles[t], sources[slot[t]], preferred_element_type=F32)
        return carry

    lax.fori_loop(0, (live + (UNROLL - 1)) >> 3, group, 0)
    mine[...] = acc[pl.ds(0, half)]
    theirs[...] = acc[pl.ds(half, half)].astype(BF16)


def aggregate(dst, slot, count, core, tiles, sources):
    half = 32
    d_in = sources.shape[-1]
    return pl.pallas_call(
        aggregate_kernel,
        out_shape=(
            jax.ShapeDtypeStruct((half, BLK, d_in), F32),
            jax.ShapeDtypeStruct((half, BLK, d_in), BF16),
        ),
        in_specs=[SMEM, SMEM, SMEM, SMEM, VMEM, VMEM],
        out_specs=(VMEM, VMEM),
        scratch_shapes=[pltpu.VMEM((2 * half + 1, BLK, d_in), F32)],
        compiler_params=pltpu.CompilerParams(vmem_limit_bytes=32 * 1024 * 1024),
        name="aggregate_tiles",
    )(dst, slot, count, core, tiles, sources)


def layer_kernel(terms, weight, cotangent, out, grad):
    total = terms[0].astype(F32)
    for i in range(1, terms.shape[0]):
        total = total + terms[i].astype(F32)
    aggregated = total.astype(BF16)
    pre = jnp.dot(aggregated, weight[...], preferred_element_type=F32)
    sig = jax.nn.sigmoid(pre)
    out[...] = (pre * sig).astype(BF16)
    grad_pre = (cotangent[...].astype(F32) * sig * (1.0 + pre * (1.0 - sig))).astype(BF16)
    for h in range(2):
        grad[h] = lax.dot_general(
            aggregated,
            grad_pre[:, h * 128 : (h + 1) * 128],
            (((0,), (0,)), ((), ())),
            preferred_element_type=F32,
        )


def layer(terms, weight, cotangent):
    return pl.pallas_call(
        layer_kernel,
        out_shape=(
            jax.ShapeDtypeStruct(cotangent.shape, BF16),
            jax.ShapeDtypeStruct((2, BLK, 128), F32),
        ),
        in_specs=[VMEM, VMEM, VMEM],
        out_specs=(VMEM, VMEM),
        name="layer",
    )(terms, weight, cotangent)


def exchange(a, axis):
    return lax.all_to_all(a, axis, 0, 0, tiled=True)


def body(x_feat, weight, tile_values, tile_dst, tile_slot, src_blocks, tile_count, cotangent):
    d_in = x_feat.shape[1]
    xs, ys, cores, cols = SIZES
    with jax.named_scope("ask"):
        listed = jnp.pad(src_blocks, ((0, 0), (0, 126))).reshape(cols, 1, 128)
        asked = exchange(listed, "col")
    with jax.named_scope("pick"):
        picked = pick(asked, x_feat)
    with jax.named_scope("sources"):
        sources = exchange(picked.reshape(cols, 2 * BLK, d_in), "col")
        sources = sources.reshape(cols * 2, BLK, d_in)
    with jax.named_scope("aggregate"):
        core = lax.axis_index("core").astype(jnp.int32).reshape(1)
        mine, theirs = aggregate(tile_dst, tile_slot, tile_count, core, tile_values, sources)
    with jax.named_scope("sum_core"):
        other = lax.ppermute(theirs, "core", [(0, 1), (1, 0)])
        summed = (mine + other.astype(F32)).astype(BF16)
    with jax.named_scope("sum_x"):
        got = exchange(summed.reshape(xs, ys * BLK, d_in), "x")
        summed = jnp.sum(got.astype(F32), axis=0).astype(BF16)
    with jax.named_scope("sum_y"):
        terms = exchange(summed.reshape(ys, BLK, d_in), "y")
    with jax.named_scope("layer"):
        layer_out, grad = layer(terms, weight, cotangent)
    with jax.named_scope("grad_row"):
        part = jnp.sum(exchange(grad.reshape(64, 4, 128), ROW), axis=0)
    with jax.named_scope("grad_col"):
        part = jnp.sum(exchange(jnp.broadcast_to(part[None], (cols, 4, 128)), "col"), axis=0)
    with jax.named_scope("grad_all"):
        whole = exchange(jnp.broadcast_to(part[None], (64, 4, 128)), ROW)
        whole = whole.reshape(2, BLK, 128)
        weight_grad = jnp.concatenate([whole[0], whole[1]], axis=1)
    return (layer_out, weight_grad)


def solution(mesh):
    grid = Mesh(mesh.devices.reshape(SIZES), AXES)
    return jax.shard_map(
        body,
        mesh=grid,
        in_specs=(
            P(AXES, None),
            P(),
            P(AXES, None, None),
            P(AXES),
            P(AXES),
            P(AXES, None),
            P(AXES),
            P(AXES, None),
        ),
        out_specs=(P(AXES, None), P()),
        check_vma=False,
    )
```

time: 738 us -> 157 us (0.21)
  waiting for transfers between devices: 688 us -> 29.4 us
  blocking collectives: 0 us -> 105 us
  local copies, waits for them, and re-layouts: 19 us -> 0.99 us
  matrix products: 15.2 us -> 0 us
  between operations: 14.5 us -> 1.36 us
  starting transfers between devices: 0.12 us -> 13.2 us
    psum x1 -> x0, waiting for transfers between devices: 464 us -> none  [body(): weight_grad = lax.psum(local_grad, ('row', 'col'))]
    reduce_scatter x1 -> x0, waiting for transfers between devices: 159 us -> none  [body(): lax.psum_scatter(partial_sum.reshape(dst_total * block, d_in), 'row', sca...]
    all_to_all x0 -> x6, blocking collectives: none -> 105 us  [exchange(): return lax.all_to_all(a, axis, 0, 0, tiled=True)]
    all_gather x1 -> x0, waiting for transfers between devices: 64.7 us -> none  [body(): whole = lax.all_gather(x_feat, 'col', axis=0, tiled=True)]
    all_to_all x0 -> x1, waiting for transfers between devices: none -> 27.1 us  [exchange(): return lax.all_to_all(a, axis, 0, 0, tiled=True)]
    dot_general x4 -> x0, matrix products: 15.2 us -> none  [the longest x1 6.01 us: body(): jnp.einsum('tij,tjf->tif', tile_values, pool[where], preferred_element_ty...]
    dot_general x2 -> x0, local copies, waits for them, and re-layouts: 10.8 us -> none  [the longest x1 6.41 us: body(): jnp.einsum('tij,tjf->tif', tile_values, pool[where], preferred_element_ty...]
    ppermute x0 -> x1, starting transfers between devices: none -> 9.6 us  [body(): other = lax.ppermute(theirs, 'core', [(0, 1), (1, 0)])]
  transfers between devices with their start and end apart: 3 -> 2, of which waited for: 3 -> 2; matrix products, arithmetic and copies ran while one was open for 0% -> 0% of each run, Pallas kernels for 0% -> 0%
where the time goes in v1:
time: 157 us
  blocking collectives  105 us (67%)
  waiting for transfers between devices  29.4 us (19%)
  starting transfers between devices  13.2 us (8%)
  Pallas kernels  5.4 us (3%)
    all_to_all x6, blocking collectives, exchange(): return lax.all_to_all(a, axis, 0, 0, tiled=True)  105 us
    all_to_all x1, waiting for transfers between devices, exchange(): return lax.all_to_all(a, axis, 0, 0, tiled=True)  27.1 us
    ppermute x1, starting transfers between devices, body(): other = lax.ppermute(theirs, 'core', [(0, 1), (1, 0)])  9.6 us
    all_to_all x1, starting transfers between devices, exchange(): return lax.all_to_all(a, axis, 0, 0, tiled=True)  3.65 us
  transfers between devices with their start and end apart: 2, of which 2 were waited for; matrix products, arithmetic and copies ran while one was open for 0% of the time, Pallas kernels for 0%

profile of v1, /device:TPU:1, one launch (start us, length us, event | category | flops | bytes accessed | tf_op | source)
XLA Modules:
  0.0 156.7 jit_solution(1567044896631167741)
XLA Ops:
  0.6 0.0 copy-start.2
  0.6 0.0 copy-start.1
  0.7 0.0 copy-start
  0.7 0.9 copy.11
  1.6 24.4 %all_to_all.35.asked = s32[12,1,128]{2,1,0:T(1,128)} all-to-all(s32[12,1,128]{2,1,0:T(1,128)S(1)} %reshape.36), channel_id=1, replica_groups=mesh['x'=4,'y'=8,'core'=2,'col'=12] {'col'}, dimensions={0} | all-to-all | bytes 12288 | tf_op jit(solution)/shard_map/ask/all_to_all | solution.py:107
  26.0 1.9 %pick_blocks.1 = bf16[12,2,128,128]{3,2,1,0:T(8,128)(2,1)} custom-call(s32[12,1,128]{2,1,0:T(1,128)} %all_to_all.35.asked, bf16[8,128,128]{2,1,0:T(8,128)(2,1)} %bitcast.13), custom_call_target="tpu_custom_call" | custom-call | tf_op jit(solution)/shard_map/pick/pick_blocks/pallas_call | solution.py:29
  27.9 3.6 %all-to-all-start.1 = ((bf16[12,256,128]{2,1,0:T(8,128)(2,1)}), bf16[12,256,128]{2,1,0:T(8,128)(2,1)S(1)}, u32[]{:S(2)}, u32[]{:S(2)}) async-start(bf16[12,256,128]{2,1,0:T(8,128)(2,1)} %bitcast.11), calls=%async_computation.1 | async-start | bytes 1572864 | tf_op jit(solution)/shard_map/sources/all_to_all | solution.py:107
  32.2 27.1 %all-to-all-done.1 = bf16[12,256,128]{2,1,0:T(8,128)(2,1)S(1)} async-done(((bf16[12,256,128]{2,1,0:T(8,128)(2,1)}), bf16[12,256,128]{2,1,0:T(8,128)(2,1)S(1)}, u32[]{:S(2)}, u32[]{:S(2)}) %all-to-all-start.1) | async-done | bytes 786464 | tf_op jit(solution)/shard_map/sources/all_to_all | solution.py:107
  59.3 0.0 copy-done.2
  59.3 0.0 copy-done.1
  59.3 0.0 copy-done
  59.3 1.5 aggregate_tiles.1
  60.9 9.6 %collective-permute-start = (bf16[32,128,128]{2,1,0:T(8,128)(2,1)S(1)}, bf16[32,128,128]{2,1,0:T(8,128)(2,1)S(1)}, u32[]{:S(2)}, u32[]{:S(2)}) collective-permute-start(bf16[32,128,128]{2,1,0:T(8,128)(2,1)S(1)} %get-tuple-element.7), channel_id=1, source_target_pairs={{0,12},{12,0},{1,13},{13,1},{2,14},{14,2},{3,15},{15,3},{4,16},{16... | collective-permute-start | bytes 3145736 | tf_op jit(solution)/shard_map/sum_core/ppermute | solution.py:125
  70.5 2.3 %collective-permute-done = bf16[32,128,128]{2,1,0:T(8,128)(2,1)S(1)} collective-permute-done((bf16[32,128,128]{2,1,0:T(8,128)(2,1)S(1)}, bf16[32,128,128]{2,1,0:T(8,128)(2,1)S(1)}, u32[]{:S(2)}, u32[]{:S(2)}) %collective-permute-start) | collective-permute-done | bytes 1048608 | tf_op jit(solution)/shard_map/sum_core/ppermute | solution.py:125
  72.7 0.4 add_convert_fusion
  73.1 19.2 %all_to_all.36 = bf16[4,1024,128]{2,1,0:T(8,128)(2,1)S(1)} all-to-all(bf16[4,1024,128]{2,1,0:T(8,128)(2,1)S(1)} %bitcast.10), channel_id=1, replica_groups=mesh['x'=4,'y'=8,'core'=2,'col'=12] {'x'}, dimensions={0} | all-to-all | bytes 2097152 | tf_op jit(solution)/shard_map/sum_x/all_to_all | solution.py:107
  92.3 0.3 reduce_sum.30
  92.6 14.1 %all_to_all.37.terms = bf16[8,128,128]{2,1,0:T(8,128)(2,1)} all-to-all(bf16[8,128,128]{2,1,0:T(8,128)(2,1)S(1)} %bitcast.12), channel_id=1, replica_groups=mesh['x'=4,'y'=8,'core'=2,'col'=12] {'y'}, dimensions={0} | all-to-all | bytes 524288 | tf_op jit(solution)/shard_map/sum_y/all_to_all | solution.py:107
  106.7 2.0 %layer.1 = (bf16[128,256]{1,0:T(8,128)(2,1)}, f32[2,128,128]{2,1,0:T(8,128)}) custom-call(bf16[8,128,128]{2,1,0:T(8,128)(2,1)} %all_to_all.37.terms, bf16[128,256]{1,0:T(8,128)(2,1)} %weight.1, bf16[128,256]{1,0:T(8,128)(2,1)} %cotangent.1), custom_call_target="tpu_custom_call" | custom-call | tf_op jit(solution)/shard_map/layer/layer/pallas_call | solution.py:94
  108.6 18.2 %all_to_all.38 = f32[64,4,128]{2,1,0:T(4,128)S(1)} all-to-all(f32[64,4,128]{2,1,0:T(4,128)} %bitcast.16), channel_id=1, replica_groups=mesh['x'=4,'y'=8,'core'=2,'col'=12] {'x','y','core'}, dimensions={0} | all-to-all | bytes 262144 | tf_op jit(solution)/shard_map/grad_row/all_to_all | solution.py:107
  126.8 0.1 reduce_sum.31
  126.9 12.6 %all_to_all.39 = f32[12,4,128]{2,1,0:T(4,128)S(1)} all-to-all(f32[12,4,128]{2,1,0:T(4,128)S(1)} %broadcast_in_dim.4), channel_id=1, replica_groups=mesh['x'=4,'y'=8,'core'=2,'col'=12] {'col'}, dimensions={0} | all-to-all | bytes 49152 | tf_op jit(solution)/shard_map/grad_col/all_to_all | solution.py:107
  139.5 16.5 %all_to_all.40 = f32[64,4,128]{2,1,0:T(4,128)S(1)} all-to-all(f32[64,4,128]{2,1,0:T(4,128)S(1)} %broadcast_in_dim.5), channel_id=1, replica_groups=mesh['x'=4,'y'=8,'core'=2,'col'=12] {'x','y','core'}, dimensions={0} | all-to-all | bytes 262144 | tf_op jit(solution)/shard_map/grad_all/all_to_all | solution.py:107
  156.0 0.7 pad_maximum_fusion
  (6 shorter events, 0.1 us)
Async XLA Ops:
  0.6 58.7 %copy-start.2 = (s32[80]{0:T(128)S(1)}, s32[80]{0:T(128)}, u32[]{:S(2)}) copy-start(s32[80]{0:T(128)} %slot.1) | copy-start | bytes 964
  0.6 58.7 %copy-start.1 = (s32[80]{0:T(128)S(1)}, s32[80]{0:T(128)}, u32[]{:S(2)}) copy-start(s32[80]{0:T(128)} %dst.1) | copy-start | bytes 964
  0.7 58.7 %copy-start = (bf16[80,128,128]{2,1,0:T(8,128)(2,1)S(1)}, bf16[80,128,128]{2,1,0:T(8,128)(2,1)}, u32[]{:S(2)}) copy-start(bf16[80,128,128]{2,1,0:T(8,128)(2,1)} %tiles.1) | copy-start | bytes 7864324
  27.9 31.4 %all-to-all-start.1 = ((bf16[12,256,128]{2,1,0:T(8,128)(2,1)}), bf16[12,256,128]{2,1,0:T(8,128)(2,1)S(1)}, u32[]{:S(2)}, u32[]{:S(2)}) async-start(bf16[12,256,128]{2,1,0:T(8,128)(2,1)} %bitcast.11), calls=%async_computation.1 | async-start | bytes 1572864 | tf_op jit(solution)/shard_map/sources/all_to_all | solution.py:107
  60.9 11.9 %collective-permute-start = (bf16[32,128,128]{2,1,0:T(8,128)(2,1)S(1)}, bf16[32,128,128]{2,1,0:T(8,128)(2,1)S(1)}, u32[]{:S(2)}, u32[]{:S(2)}) collective-permute-start(bf16[32,128,128]{2,1,0:T(8,128)(2,1)S(1)} %get-tuple-element.7), channel_id=1, source_target_pairs={{0,12},{12,0},{1,13},{13,1},{2,14},{14,2},{3,15},{15,3},{4,16},{16... | collective-permute-start | bytes 3145736 | tf_op jit(solution)/shard_map/sum_core/ppermute | solution.py:125

commit v2 on v1

--- a/solution.py
+++ b/solution.py
@@ -8,7 +8,6 @@
 BLK = 128
 UNROLL = 8
 AXES = ("x", "y", "core", "col")
-ROW = ("x", "y", "core")
 SIZES = (4, 8, 2, 12)
 
 VMEM = pl.BlockSpec(memory_space=pltpu.VMEM)
@@ -21,7 +20,7 @@
     peers, listed = out_ref.shape[0], out_ref.shape[1]
     for p in range(peers):
         for k in range(listed):
-            out_ref[p, k] = x_ref[asked[p, 0, k]]
+            out_ref[p, k] = x_ref[(asked[p, 0, 0] >> (8 * k)) & 255]
 
 
 def pick(asked, x_feat):
@@ -31,6 +30,7 @@
         out_shape=jax.ShapeDtypeStruct((peers, listed, BLK, x_feat.shape[1]), BF16),
         in_specs=[SMEM, VMEM],
         out_specs=VMEM,
+        compiler_params=pltpu.CompilerParams(vmem_limit_bytes=4 * 1024 * 1024),
         name="pick_blocks",
     )(asked, x_feat.reshape(-1, BLK, x_feat.shape[1]))
 
@@ -67,16 +67,13 @@
         in_specs=[SMEM, SMEM, SMEM, SMEM, VMEM, VMEM],
         out_specs=(VMEM, VMEM),
         scratch_shapes=[pltpu.VMEM((2 * half + 1, BLK, d_in), F32)],
-        compiler_params=pltpu.CompilerParams(vmem_limit_bytes=32 * 1024 * 1024),
+        compiler_params=pltpu.CompilerParams(vmem_limit_bytes=16 * 1024 * 1024),
         name="aggregate_tiles",
     )(dst, slot, count, core, tiles, sources)
 
 
 def layer_kernel(terms, weight, cotangent, out, grad):
-    total = terms[0].astype(F32)
-    for i in range(1, terms.shape[0]):
-        total = total + terms[i].astype(F32)
-    aggregated = total.astype(BF16)
+    aggregated = add_all(terms).astype(BF16)
     pre = jnp.dot(aggregated, weight[...], preferred_element_type=F32)
     sig = jax.nn.sigmoid(pre)
     out[...] = (pre * sig).astype(BF16)
@@ -99,6 +96,7 @@
         ),
         in_specs=[VMEM, VMEM, VMEM],
         out_specs=(VMEM, VMEM),
+        compiler_params=pltpu.CompilerParams(vmem_limit_bytes=4 * 1024 * 1024),
         name="layer",
     )(terms, weight, cotangent)
 
@@ -107,12 +105,19 @@
     return lax.all_to_all(a, axis, 0, 0, tiled=True)
 
 
+def add_all(terms):
+    total = terms[0].astype(F32)
+    for i in range(1, terms.shape[0]):
+        total = total + terms[i].astype(F32)
+    return total
+
+
 def body(x_feat, weight, tile_values, tile_dst, tile_slot, src_blocks, tile_count, cotangent):
     d_in = x_feat.shape[1]
     xs, ys, cores, cols = SIZES
     with jax.named_scope("ask"):
-        listed = jnp.pad(src_blocks, ((0, 0), (0, 126))).reshape(cols, 1, 128)
-        asked = exchange(listed, "col")
+        pair = src_blocks[:, 0] + 256 * src_blocks[:, 1]
+        asked = exchange(jnp.broadcast_to(pair[:, None, None], (cols, 1, 128)), "col")
     with jax.named_scope("pick"):
         picked = pick(asked, x_feat)
     with jax.named_scope("sources"):
@@ -126,17 +131,18 @@
         summed = (mine + other.astype(F32)).astype(BF16)
     with jax.named_scope("sum_x"):
         got = exchange(summed.reshape(xs, ys * BLK, d_in), "x")
-        summed = jnp.sum(got.astype(F32), axis=0).astype(BF16)
+        summed = add_all(got).astype(BF16)
     with jax.named_scope("sum_y"):
         terms = exchange(summed.reshape(ys, BLK, d_in), "y")
     with jax.named_scope("layer"):
         layer_out, grad = layer(terms, weight, cotangent)
-    with jax.named_scope("grad_row"):
-        part = jnp.sum(exchange(grad.reshape(64, 4, 128), ROW), axis=0)
-    with jax.named_scope("grad_col"):
-        part = jnp.sum(exchange(jnp.broadcast_to(part[None], (cols, 4, 128)), "col"), axis=0)
+    with jax.named_scope("grad_xy"):
+        part = jnp.sum(exchange(grad.reshape(32, 8, 128), ("x", "y")), axis=0)
+    with jax.named_scope("grad_core_col"):
+        part = jnp.broadcast_to(part[None], (24, 8, 128))
+        part = jnp.sum(exchange(part, ("core", "col")), axis=0)
     with jax.named_scope("grad_all"):
-        whole = exchange(jnp.broadcast_to(part[None], (64, 4, 128)), ROW)
+        whole = exchange(jnp.broadcast_to(part[None], (32, 8, 128)), ("x", "y"))
         whole = whole.reshape(2, BLK, 128)
         weight_grad = jnp.concatenate([whole[0], whole[1]], axis=1)
     return (layer_out, weight_grad)

time: 157 us -> 154 us (0.981)
  blocking collectives: 105 us -> 102 us
    all_to_all x6, blocking collectives: 105 us -> 102 us  [exchange(): return lax.all_to_all(a, axis, 0, 0, tiled=True)]
where the time goes in v2:
time: 154 us; the launch traced here: 153 us
  blocking collectives  102 us (66%)
  waiting for transfers between devices  29.4 us (19%)
  starting transfers between devices  11.8 us (8%)
  Pallas kernels  4.62 us (3%)
  other arithmetic  2.06 us (1%)
    all_to_all x6, blocking collectives, exchange(): return lax.all_to_all(a, axis, 0, 0, tiled=True)  102 us
    all_to_all x1, waiting for transfers between devices, exchange(): return lax.all_to_all(a, axis, 0, 0, tiled=True)  27.2 us
    ppermute x1, starting transfers between devices, body(): other = lax.ppermute(theirs, 'core', [(0, 1), (1, 0)])  8.17 us
    all_to_all x1, starting transfers between devices, exchange(): return lax.all_to_all(a, axis, 0, 0, tiled=True)  3.65 us
  transfers between devices with their start and end apart: 2, of which 2 were waited for; matrix products, arithmetic and copies ran while one was open for 0% of the time, Pallas kernels for 0%

profile of v2, /device:TPU:1, one launch (start us, length us, event | category | flops | bytes accessed | tf_op | source)
XLA Modules:
  0.0 152.7 jit_solution(5529595946227019699)
XLA Ops:
  0.6 0.0 copy-start
  0.6 0.9 add_bitcast_fusion
  1.5 0.1 broadcast_in_dim.6
  1.6 24.4 %all_to_all.35.asked = s32[12,1,128]{2,1,0:T(1,128)S(1)} all-to-all(s32[12,1,128]{2,1,0:T(1,128)S(1)} %broadcast_in_dim.6), channel_id=1, replica_groups=mesh['x'=4,'y'=8,'core'=2,'col'=12] {'col'}, dimensions={0} | all-to-all | bytes 12288 | tf_op jit(solution)/shard_map/ask/all_to_all | solution.py:105
  26.0 0.0 copy-start.1
  26.0 0.9 copy-done.1
  26.9 0.0 copy-start.4
  26.9 0.0 copy-start.5
  26.9 1.6 %pick_blocks.1 = bf16[12,2,128,128]{3,2,1,0:T(8,128)(2,1)} custom-call(s32[12,1,128]{2,1,0:T(1,128)S(1)} %all_to_all.35.asked, bf16[8,128,128]{2,1,0:T(8,128)(2,1)S(1)} %bitcast.14), custom_call_target="tpu_custom_call" | custom-call | tf_op jit(solution)/shard_map/pick/pick_blocks/pallas_call | solution.py:28
  28.5 3.6 %all-to-all-start.1 = ((bf16[12,256,128]{2,1,0:T(8,128)(2,1)}), bf16[12,256,128]{2,1,0:T(8,128)(2,1)S(1)}, u32[]{:S(2)}, u32[]{:S(2)}) async-start(bf16[12,256,128]{2,1,0:T(8,128)(2,1)} %bitcast.3), calls=%async_computation.1 | async-start | bytes 1572864 | tf_op jit(solution)/shard_map/sources/all_to_all | solution.py:105
  32.8 27.2 %all-to-all-done.1 = bf16[12,256,128]{2,1,0:T(8,128)(2,1)S(1)} async-done(((bf16[12,256,128]{2,1,0:T(8,128)(2,1)}), bf16[12,256,128]{2,1,0:T(8,128)(2,1)S(1)}, u32[]{:S(2)}, u32[]{:S(2)}) %all-to-all-start.1) | async-done | bytes 786464 | tf_op jit(solution)/shard_map/sources/all_to_all | solution.py:105
  60.0 0.0 copy-done
  60.0 0.0 copy-done.4
  60.0 0.0 copy-done.5
  60.0 2.2 %aggregate_tiles.1 = (f32[32,128,128]{2,1,0:T(8,128)S(1)}, bf16[32,128,128]{2,1,0:T(8,128)(2,1)S(1)}) custom-call(s32[80]{0:T(128)S(1)} %copy-done.4, s32[80]{0:T(128)S(1)} %copy-done.5, s32[1]{0:T(128)S(6)} %copy.10.count, s32[1]{0:T(128)} %bitcast.core, bf16[80,128,128]{2,1,0:T(8,128)(2,1)S(1)} %copy-done, bf16[24,128,128]{2,1,0:T(8,128)(2,1)S(1)} %bitcast.13), custom_call_target="tpu_custom_call" | custom-call | tf_op jit(solution)/shard_map/aggregate/aggregate_tiles/pallas_call | solution.py:61
  62.2 8.2 %collective-permute-start = (bf16[32,128,128]{2,1,0:T(8,128)(2,1)S(1)}, bf16[32,128,128]{2,1,0:T(8,128)(2,1)S(1)}, u32[]{:S(2)}, u32[]{:S(2)}) collective-permute-start(bf16[32,128,128]{2,1,0:T(8,128)(2,1)S(1)} %get-tuple-element.7), channel_id=1, source_target_pairs={{0,12},{12,0},{1,13},{13,1},{2,14},{14,2},{3,15},{15,3},{4,16},{16... | collective-permute-start | bytes 3145736 | tf_op jit(solution)/shard_map/sum_core/ppermute | solution.py:130
  70.4 2.3 %collective-permute-done = bf16[32,128,128]{2,1,0:T(8,128)(2,1)S(1)} collective-permute-done((bf16[32,128,128]{2,1,0:T(8,128)(2,1)S(1)}, bf16[32,128,128]{2,1,0:T(8,128)(2,1)S(1)}, u32[]{:S(2)}, u32[]{:S(2)}) %collective-permute-start) | collective-permute-done | bytes 1048608 | tf_op jit(solution)/shard_map/sum_core/ppermute | solution.py:130
  72.7 0.3 add_convert_fusion
  73.0 0.0 copy-start.2
  73.0 0.0 copy-start.3
  73.1 18.9 %all_to_all.36 = bf16[4,1024,128]{2,1,0:T(8,128)(2,1)S(1)} all-to-all(bf16[4,1024,128]{2,1,0:T(8,128)(2,1)S(1)} %bitcast.16), channel_id=1, replica_groups=mesh['x'=4,'y'=8,'core'=2,'col'=12] {'x'}, dimensions={0} | all-to-all | bytes 2097152 | tf_op jit(solution)/shard_map/sum_x/all_to_all | solution.py:105
  91.9 0.1 add_convert_fusion.1
  92.1 16.2 %all_to_all.37.terms = bf16[8,128,128]{2,1,0:T(8,128)(2,1)S(1)} all-to-all(bf16[8,128,128]{2,1,0:T(8,128)(2,1)S(1)} %bitcast.17), channel_id=1, replica_groups=mesh['x'=4,'y'=8,'core'=2,'col'=12] {'y'}, dimensions={0} | all-to-all | bytes 524288 | tf_op jit(solution)/shard_map/sum_y/all_to_all | solution.py:105
  108.3 0.0 copy-done.2
  108.3 0.0 copy-done.3
  108.3 0.8 layer.1
  109.1 12.6 %all_to_all.38 = f32[32,8,128]{2,1,0:T(8,128)S(1)} all-to-all(f32[32,8,128]{2,1,0:T(8,128)S(1)} %bitcast.15), channel_id=1, replica_groups=mesh['x'=4,'y'=8,'core'=2,'col'=12] {'x','y'}, dimensions={0} | all-to-all | bytes 262144 | tf_op jit(solution)/shard_map/grad_xy/all_to_all | solution.py:105
  121.7 17.8 %all_to_all.39 = f32[24,8,128]{2,1,0:T(8,128)S(1)} all-to-all(f32[24,8,128]{2,1,0:T(8,128)S(1)} %broadcast_in_dim.7), channel_id=1, replica_groups=mesh['x'=4,'y'=8,'core'=2,'col'=12] {'core','col'}, dimensions={0} | all-to-all | bytes 196608 | tf_op jit(solution)/shard_map/grad_core_col/all_to_all | solution.py:105
  139.6 12.4 %all_to_all.40 = f32[32,8,128]{2,1,0:T(8,128)S(1)} all-to-all(f32[32,8,128]{2,1,0:T(8,128)S(1)} %broadcast_in_dim.8), channel_id=1, replica_groups=mesh['x'=4,'y'=8,'core'=2,'col'=12] {'x','y'}, dimensions={0} | all-to-all | bytes 262144 | tf_op jit(solution)/shard_map/grad_all/all_to_all | solution.py:105
  152.0 0.7 pad_maximum_fusion
  (5 shorter events, 0.1 us)
Async XLA Ops:
  0.6 59.4 %copy-start = (bf16[80,128,128]{2,1,0:T(8,128)(2,1)S(1)}, bf16[80,128,128]{2,1,0:T(8,128)(2,1)}, u32[]{:S(2)}) copy-start(bf16[80,128,128]{2,1,0:T(8,128)(2,1)} %tiles.1) | copy-start | bytes 7864324
  26.0 1.0 copy-start.1
  26.9 33.0 %copy-start.4 = (s32[80]{0:T(128)S(1)}, s32[80]{0:T(128)}, u32[]{:S(2)}) copy-start(s32[80]{0:T(128)} %dst.1) | copy-start | bytes 964
  26.9 33.1 %copy-start.5 = (s32[80]{0:T(128)S(1)}, s32[80]{0:T(128)}, u32[]{:S(2)}) copy-start(s32[80]{0:T(128)} %slot.1) | copy-start | bytes 964
  28.5 31.5 %all-to-all-start.1 = ((bf16[12,256,128]{2,1,0:T(8,128)(2,1)}), bf16[12,256,128]{2,1,0:T(8,128)(2,1)S(1)}, u32[]{:S(2)}, u32[]{:S(2)}) async-start(bf16[12,256,128]{2,1,0:T(8,128)(2,1)} %bitcast.3), calls=%async_computation.1 | async-start | bytes 1572864 | tf_op jit(solution)/shard_map/sources/all_to_all | solution.py:105
  62.2 10.4 %collective-permute-start = (bf16[32,128,128]{2,1,0:T(8,128)(2,1)S(1)}, bf16[32,128,128]{2,1,0:T(8,128)(2,1)S(1)}, u32[]{:S(2)}, u32[]{:S(2)}) collective-permute-start(bf16[32,128,128]{2,1,0:T(8,128)(2,1)S(1)} %get-tuple-element.7), channel_id=1, source_target_pairs={{0,12},{12,0},{1,13},{13,1},{2,14},{14,2},{3,15},{15,3},{4,16},{16... | collective-permute-start | bytes 3145736 | tf_op jit(solution)/shard_map/sum_core/ppermute | solution.py:130
  73.0 35.3 %copy-start.2 = (bf16[128,256]{1,0:T(8,128)(2,1)S(1)}, bf16[128,256]{1,0:T(8,128)(2,1)}, u32[]{:S(2)}) copy-start(bf16[128,256]{1,0:T(8,128)(2,1)} %weight.1) | copy-start | bytes 196612
  73.0 35.3 %copy-start.3 = (bf16[128,256]{1,0:T(8,128)(2,1)S(1)}, bf16[128,256]{1,0:T(8,128)(2,1)}, u32[]{:S(2)}) copy-start(bf16[128,256]{1,0:T(8,128)(2,1)} %cotangent.1) | copy-start | bytes 196612

commit v3 on v2

--- a/solution.py
+++ b/solution.py
@@ -6,9 +6,9 @@
 from jax.sharding import Mesh, PartitionSpec as P
 
 BLK = 128
-UNROLL = 8
-AXES = ("x", "y", "core", "col")
-SIZES = (4, 8, 2, 12)
+UNROLL = 20
+AXES = ("x", "far", "near", "core", "col")
+SIZES = (4, 4, 2, 2, 12)
 
 VMEM = pl.BlockSpec(memory_space=pltpu.VMEM)
 SMEM = pl.BlockSpec(memory_space=pltpu.SMEM)
@@ -24,19 +24,18 @@
 
 
 def pick(asked, x_feat):
-    peers, listed = SIZES[3], 2
+    peers, listed = SIZES[4], 2
     return pl.pallas_call(
         pick_kernel,
         out_shape=jax.ShapeDtypeStruct((peers, listed, BLK, x_feat.shape[1]), BF16),
         in_specs=[SMEM, VMEM],
         out_specs=VMEM,
-        compiler_params=pltpu.CompilerParams(vmem_limit_bytes=4 * 1024 * 1024),
         name="pick_blocks",
     )(asked, x_feat.reshape(-1, BLK, x_feat.shape[1]))
 
 
-def aggregate_kernel(dst, slot, count, core, tiles, sources, mine, theirs, acc):
-    half = mine.shape[0]
+def aggregate_kernel(dst, slot, count, core, tiles, sources, acc, theirs):
+    half = theirs.shape[0]
     live = count[0]
     me = core[0]
     acc[...] = jnp.zeros_like(acc)
@@ -45,13 +44,13 @@
         for u in range(UNROLL):
             t = g * UNROLL + u
             d = dst[t]
-            place = ((d & 1) ^ me) * half + (d >> 1)
+            xy = (d & 0x30) | ((d & 2) << 2) | ((d & 0xC) >> 1)
+            place = ((d & 1) ^ me) * half + (xy >> 1)
             place = jnp.where(t < live, place, 2 * half)
             acc[place] += jnp.dot(tiles[t], sources[slot[t]], preferred_element_type=F32)
         return carry
 
-    lax.fori_loop(0, (live + (UNROLL - 1)) >> 3, group, 0)
-    mine[...] = acc[pl.ds(0, half)]
+    lax.fori_loop(0, lax.div(live + (UNROLL - 1), UNROLL), group, 0)
     theirs[...] = acc[pl.ds(half, half)].astype(BF16)
 
 
@@ -61,12 +60,11 @@
     return pl.pallas_call(
         aggregate_kernel,
         out_shape=(
-            jax.ShapeDtypeStruct((half, BLK, d_in), F32),
+            jax.ShapeDtypeStruct((2 * half + 1, BLK, d_in), F32),
             jax.ShapeDtypeStruct((half, BLK, d_in), BF16),
         ),
         in_specs=[SMEM, SMEM, SMEM, SMEM, VMEM, VMEM],
         out_specs=(VMEM, VMEM),
-        scratch_shapes=[pltpu.VMEM((2 * half + 1, BLK, d_in), F32)],
         compiler_params=pltpu.CompilerParams(vmem_limit_bytes=16 * 1024 * 1024),
         name="aggregate_tiles",
     )(dst, slot, count, core, tiles, sources)
@@ -114,7 +112,7 @@
 
 def body(x_feat, weight, tile_values, tile_dst, tile_slot, src_blocks, tile_count, cotangent):
     d_in = x_feat.shape[1]
-    xs, ys, cores, cols = SIZES
+    xs, fars, nears, cores, cols = SIZES
     with jax.named_scope("ask"):
         pair = src_blocks[:, 0] + 256 * src_blocks[:, 1]
         asked = exchange(jnp.broadcast_to(pair[:, None, None], (cols, 1, 128)), "col")
@@ -128,21 +126,21 @@
         mine, theirs = aggregate(tile_dst, tile_slot, tile_count, core, tile_values, sources)
     with jax.named_scope("sum_core"):
         other = lax.ppermute(theirs, "core", [(0, 1), (1, 0)])
-        summed = (mine + other.astype(F32)).astype(BF16)
-    with jax.named_scope("sum_x"):
-        got = exchange(summed.reshape(xs, ys * BLK, d_in), "x")
+        summed = (mine[: other.shape[0]] + other.astype(F32)).astype(BF16)
+    with jax.named_scope("sum_x_near"):
+        got = exchange(summed.reshape(xs * nears, fars * BLK, d_in), ("x", "near"))
         summed = add_all(got).astype(BF16)
-    with jax.named_scope("sum_y"):
-        terms = exchange(summed.reshape(ys, BLK, d_in), "y")
+    with jax.named_scope("sum_far"):
+        terms = exchange(summed.reshape(fars, BLK, d_in), "far")
     with jax.named_scope("layer"):
         layer_out, grad = layer(terms, weight, cotangent)
     with jax.named_scope("grad_xy"):
-        part = jnp.sum(exchange(grad.reshape(32, 8, 128), ("x", "y")), axis=0)
+        part = jnp.sum(exchange(grad.reshape(32, 8, 128), ("x", "far", "near")), axis=0)
     with jax.named_scope("grad_core_col"):
         part = jnp.broadcast_to(part[None], (24, 8, 128))
         part = jnp.sum(exchange(part, ("core", "col")), axis=0)
     with jax.named_scope("grad_all"):
-        whole = exchange(jnp.broadcast_to(part[None], (32, 8, 128)), ("x", "y"))
+        whole = exchange(jnp.broadcast_to(part[None], (32, 8, 128)), ("x", "far", "near"))
         whole = whole.reshape(2, BLK, 128)
         weight_grad = jnp.concatenate([whole[0], whole[1]], axis=1)
     return (layer_out, weight_grad)

time: 154 us -> 152 us (0.987)
    all_to_all x6, blocking collectives: 102 us -> 101 us  [exchange(): return lax.all_to_all(a, axis, 0, 0, tiled=True)]
where the time goes in v3:
time: 152 us; the launch traced here: 150 us
  blocking collectives  101 us (66%)
  waiting for transfers between devices  29.4 us (19%)
  starting transfers between devices  11.9 us (8%)
  Pallas kernels  5.02 us (3%)
  other arithmetic  2.04 us (1%)
    all_to_all x6, blocking collectives, exchange(): return lax.all_to_all(a, axis, 0, 0, tiled=True)  101 us
    all_to_all x1, waiting for transfers between devices, exchange(): return lax.all_to_all(a, axis, 0, 0, tiled=True)  27.1 us
    ppermute x1, starting transfers between devices, body(): other = lax.ppermute(theirs, 'core', [(0, 1), (1, 0)])  8.2 us
    all_to_all x1, starting transfers between devices, exchange(): return lax.all_to_all(a, axis, 0, 0, tiled=True)  3.65 us
  transfers between devices with their start and end apart: 2, of which 2 were waited for; matrix products, arithmetic and copies ran while one was open for 0% of the time, Pallas kernels for 0%

profile of v3, /device:TPU:1, one launch (start us, length us, event | category | flops | bytes accessed | tf_op | source)
XLA Modules:
  0.0 150.3 jit_solution(14820769963313693380)
XLA Ops:
  0.6 0.0 copy-start.4
  0.6 0.0 copy-start.3
  0.7 0.0 copy-start
  0.7 0.9 add_bitcast_fusion
  1.5 0.1 broadcast_in_dim.6
  1.6 24.4 %all_to_all.35.asked = s32[12,1,128]{2,1,0:T(1,128)} all-to-all(s32[12,1,128]{2,1,0:T(1,128)S(1)} %broadcast_in_dim.6), channel_id=1, replica_groups=mesh['x'=4,'far'=4,'near'=2,'core'=2,'col'=12] {'col'}, dimensions={0} | all-to-all | bytes 12288 | tf_op jit(solution)/shard_map/ask/all_to_all | solution.py:103
  26.0 1.9 %pick_blocks.1 = bf16[12,2,128,128]{3,2,1,0:T(8,128)(2,1)} custom-call(s32[12,1,128]{2,1,0:T(1,128)} %all_to_all.35.asked, bf16[8,128,128]{2,1,0:T(8,128)(2,1)} %bitcast.18), custom_call_target="tpu_custom_call" | custom-call | tf_op jit(solution)/shard_map/pick/pick_blocks/pallas_call | solution.py:28
  27.9 3.6 %all-to-all-start.1 = ((bf16[12,256,128]{2,1,0:T(8,128)(2,1)}), bf16[12,256,128]{2,1,0:T(8,128)(2,1)S(1)}, u32[]{:S(2)}, u32[]{:S(2)}) async-start(bf16[12,256,128]{2,1,0:T(8,128)(2,1)} %bitcast.16), calls=%async_computation.1 | async-start | bytes 1572864 | tf_op jit(solution)/shard_map/sources/all_to_all | solution.py:103
  32.2 27.1 %all-to-all-done.1 = bf16[12,256,128]{2,1,0:T(8,128)(2,1)S(1)} async-done(((bf16[12,256,128]{2,1,0:T(8,128)(2,1)}), bf16[12,256,128]{2,1,0:T(8,128)(2,1)S(1)}, u32[]{:S(2)}, u32[]{:S(2)}) %all-to-all-start.1) | async-done | bytes 786464 | tf_op jit(solution)/shard_map/sources/all_to_all | solution.py:103
  59.3 0.0 copy-done.4
  59.3 0.0 copy-done.3
  59.3 0.0 copy-done
  59.3 2.3 %aggregate_tiles.1 = (f32[65,128,128]{2,1,0:T(8,128)S(1)}, bf16[32,128,128]{2,1,0:T(8,128)(2,1)S(1)}) custom-call(s32[80]{0:T(128)S(1)} %copy-done.3, s32[80]{0:T(128)S(1)} %copy-done.4, s32[1]{0:T(128)S(6)} %copy.10.count, s32[1]{0:T(128)} %bitcast.core, bf16[80,128,128]{2,1,0:T(8,128)(2,1)S(1)} %copy-done, bf16[24,128,128]{2,1,0:T(8,128)(2,1)S(1)} %bitcast.13), custom_call_target="tpu_custom_call" | custom-call | tf_op jit(solution)/shard_map/aggregate/aggregate_tiles/pallas_call | solution.py:60
  61.6 8.2 %collective-permute-start = (bf16[32,128,128]{2,1,0:T(8,128)(2,1)S(1)}, bf16[32,128,128]{2,1,0:T(8,128)(2,1)S(1)}, u32[]{:S(2)}, u32[]{:S(2)}) collective-permute-start(bf16[32,128,128]{2,1,0:T(8,128)(2,1)S(1)} %get-tuple-element.7), channel_id=1, source_target_pairs={{0,12},{12,0},{1,13},{13,1},{2,14},{14,2},{3,15},{15,3},{4,16},{16... | collective-permute-start | bytes 3145736 | tf_op jit(solution)/shard_map/sum_core/ppermute | solution.py:128
  69.9 2.3 %collective-permute-done = bf16[32,128,128]{2,1,0:T(8,128)(2,1)S(1)} collective-permute-done((bf16[32,128,128]{2,1,0:T(8,128)(2,1)S(1)}, bf16[32,128,128]{2,1,0:T(8,128)(2,1)S(1)}, u32[]{:S(2)}, u32[]{:S(2)}) %collective-permute-start) | collective-permute-done | bytes 1048608 | tf_op jit(solution)/shard_map/sum_core/ppermute | solution.py:128
  72.1 0.3 add_convert_fusion
  72.4 0.0 copy-start.1
  72.5 0.0 copy-start.2
  72.5 20.5 %all_to_all.36 = bf16[8,512,128]{2,1,0:T(8,128)(2,1)S(1)} all-to-all(bf16[8,512,128]{2,1,0:T(8,128)(2,1)S(1)} %bitcast.15), channel_id=1, replica_groups=mesh['x'=4,'far'=4,'near'=2,'core'=2,'col'=12] {'x','near'}, dimensions={0} | all-to-all | bytes 2097152 | tf_op jit(solution)/shard_map/sum_x_near/all_to_all | solution.py:103
  93.0 0.1 add_convert_fusion.1
  93.1 12.9 %all_to_all.37.terms = bf16[4,128,128]{2,1,0:T(8,128)(2,1)S(1)} all-to-all(bf16[4,128,128]{2,1,0:T(8,128)(2,1)S(1)} %bitcast.17), channel_id=1, replica_groups=mesh['x'=4,'far'=4,'near'=2,'core'=2,'col'=12] {'far'}, dimensions={0} | all-to-all | bytes 262144 | tf_op jit(solution)/shard_map/sum_far/all_to_all | solution.py:103
  106.0 0.0 copy-done.1
  106.0 0.0 copy-done.2
  106.0 0.8 layer.1
  106.9 13.1 %all_to_all.38 = f32[32,8,128]{2,1,0:T(8,128)S(1)} all-to-all(f32[32,8,128]{2,1,0:T(8,128)S(1)} %bitcast.14), channel_id=1, replica_groups=mesh['x'=4,'far'=4,'near'=2,'core'=2,'col'=12] {'x','far','near'}, dimensions={0} | all-to-all | bytes 262144 | tf_op jit(solution)/shard_map/grad_xy/all_to_all | solution.py:103
  120.0 17.4 %all_to_all.39 = f32[24,8,128]{2,1,0:T(8,128)S(1)} all-to-all(f32[24,8,128]{2,1,0:T(8,128)S(1)} %broadcast_in_dim.7), channel_id=1, replica_groups=mesh['x'=4,'far'=4,'near'=2,'core'=2,'col'=12] {'core','col'}, dimensions={0} | all-to-all | bytes 196608 | tf_op jit(solution)/shard_map/grad_core_col/all_to_all | solution.py:103
  137.4 12.3 %all_to_all.40 = f32[32,8,128]{2,1,0:T(8,128)S(1)} all-to-all(f32[32,8,128]{2,1,0:T(8,128)S(1)} %broadcast_in_dim.8), channel_id=1, replica_groups=mesh['x'=4,'far'=4,'near'=2,'core'=2,'col'=12] {'x','far','near'}, dimensions={0} | all-to-all | bytes 262144 | tf_op jit(solution)/shard_map/grad_all/all_to_all | solution.py:103
  149.7 0.7 pad_maximum_fusion
  (5 shorter events, 0.1 us)
Async XLA Ops:
  0.6 58.7 %copy-start.4 = (s32[80]{0:T(128)S(1)}, s32[80]{0:T(128)}, u32[]{:S(2)}) copy-start(s32[80]{0:T(128)} %slot.1) | copy-start | bytes 964
  0.6 58.7 %copy-start.3 = (s32[80]{0:T(128)S(1)}, s32[80]{0:T(128)}, u32[]{:S(2)}) copy-start(s32[80]{0:T(128)} %dst.1) | copy-start | bytes 964
  0.7 58.7 %copy-start = (bf16[80,128,128]{2,1,0:T(8,128)(2,1)S(1)}, bf16[80,128,128]{2,1,0:T(8,128)(2,1)}, u32[]{:S(2)}) copy-start(bf16[80,128,128]{2,1,0:T(8,128)(2,1)} %tiles.1) | copy-start | bytes 7864324
  27.9 31.4 %all-to-all-start.1 = ((bf16[12,256,128]{2,1,0:T(8,128)(2,1)}), bf16[12,256,128]{2,1,0:T(8,128)(2,1)S(1)}, u32[]{:S(2)}, u32[]{:S(2)}) async-start(bf16[12,256,128]{2,1,0:T(8,128)(2,1)} %bitcast.16), calls=%async_computation.1 | async-start | bytes 1572864 | tf_op jit(solution)/shard_map/sources/all_to_all | solution.py:103
  61.6 10.5 %collective-permute-start = (bf16[32,128,128]{2,1,0:T(8,128)(2,1)S(1)}, bf16[32,128,128]{2,1,0:T(8,128)(2,1)S(1)}, u32[]{:S(2)}, u32[]{:S(2)}) collective-permute-start(bf16[32,128,128]{2,1,0:T(8,128)(2,1)S(1)} %get-tuple-element.7), channel_id=1, source_target_pairs={{0,12},{12,0},{1,13},{13,1},{2,14},{14,2},{3,15},{15,3},{4,16},{16... | collective-permute-start | bytes 3145736 | tf_op jit(solution)/shard_map/sum_core/ppermute | solution.py:128
  72.4 33.6 %copy-start.1 = (bf16[128,256]{1,0:T(8,128)(2,1)S(1)}, bf16[128,256]{1,0:T(8,128)(2,1)}, u32[]{:S(2)}) copy-start(bf16[128,256]{1,0:T(8,128)(2,1)} %weight.1) | copy-start | bytes 196612
  72.5 33.6 %copy-start.2 = (bf16[128,256]{1,0:T(8,128)(2,1)S(1)}, bf16[128,256]{1,0:T(8,128)(2,1)}, u32[]{:S(2)}) copy-start(bf16[128,256]{1,0:T(8,128)(2,1)} %cotangent.1) | copy-start | bytes 196612

commit v4 on v3

--- a/solution.py
+++ b/solution.py
@@ -82,7 +82,7 @@
             grad_pre[:, h * 128 : (h + 1) * 128],
             (((0,), (0,)), ((), ())),
             preferred_element_type=F32,
-        )
+        ).astype(BF16)
 
 
 def layer(terms, weight, cotangent):
@@ -90,7 +90,7 @@
         layer_kernel,
         out_shape=(
             jax.ShapeDtypeStruct(cotangent.shape, BF16),
-            jax.ShapeDtypeStruct((2, BLK, 128), F32),
+            jax.ShapeDtypeStruct((2, BLK, 128), BF16),
         ),
         in_specs=[VMEM, VMEM, VMEM],
         out_specs=(VMEM, VMEM),
@@ -135,7 +135,7 @@
     with jax.named_scope("layer"):
         layer_out, grad = layer(terms, weight, cotangent)
     with jax.named_scope("grad_xy"):
-        part = jnp.sum(exchange(grad.reshape(32, 8, 128), ("x", "far", "near")), axis=0)
+        part = add_all(exchange(grad.reshape(32, 8, 128), ("x", "far", "near")))
     with jax.named_scope("grad_core_col"):
         part = jnp.broadcast_to(part[None], (24, 8, 128))
         part = jnp.sum(exchange(part, ("core", "col")), axis=0)

time: 152 us -> 151 us (level)
  no operation moved by 1% of the time
where the time goes in v4:
time: 151 us; the launch traced here: 150 us
  blocking collectives  100 us (66%)
  waiting for transfers between devices  29.4 us (19%)
  starting transfers between devices  12.5 us (8%)
  Pallas kernels  3.98 us (3%)
  other arithmetic  2.04 us (1%)
    all_to_all x6, blocking collectives, exchange(): return lax.all_to_all(a, axis, 0, 0, tiled=True)  100 us
    all_to_all x1, waiting for transfers between devices, exchange(): return lax.all_to_all(a, axis, 0, 0, tiled=True)  27.1 us
    ppermute x1, starting transfers between devices, body(): other = lax.ppermute(theirs, 'core', [(0, 1), (1, 0)])  8.89 us
    all_to_all x1, starting transfers between devices, exchange(): return lax.all_to_all(a, axis, 0, 0, tiled=True)  3.65 us
  transfers between devices with their start and end apart: 2, of which 2 were waited for; matrix products, arithmetic and copies ran while one was open for 0% of the time, Pallas kernels for 0%

profile of v4, /device:TPU:1, one launch (start us, length us, event | category | flops | bytes accessed | tf_op | source)
XLA Modules:
  0.0 149.8 jit_solution(11777271270741308399)
XLA Ops:
  0.6 0.0 copy-start.4
  0.6 0.0 copy-start.3
  0.7 0.0 copy-start
  0.7 0.9 add_bitcast_fusion.1
  1.5 0.1 broadcast_in_dim.8
  1.6 24.4 %all_to_all.35.asked = s32[12,1,128]{2,1,0:T(1,128)} all-to-all(s32[12,1,128]{2,1,0:T(1,128)S(1)} %broadcast_in_dim.8), channel_id=1, replica_groups=mesh['x'=4,'far'=4,'near'=2,'core'=2,'col'=12] {'col'}, dimensions={0} | all-to-all | bytes 12288 | tf_op jit(solution)/shard_map/ask/all_to_all | solution.py:103
  26.0 1.9 %pick_blocks.1 = bf16[12,2,128,128]{3,2,1,0:T(8,128)(2,1)} custom-call(s32[12,1,128]{2,1,0:T(1,128)} %all_to_all.35.asked, bf16[8,128,128]{2,1,0:T(8,128)(2,1)} %bitcast.20), custom_call_target="tpu_custom_call" | custom-call | tf_op jit(solution)/shard_map/pick/pick_blocks/pallas_call | solution.py:28
  27.9 3.6 %all-to-all-start.1 = ((bf16[12,256,128]{2,1,0:T(8,128)(2,1)}), bf16[12,256,128]{2,1,0:T(8,128)(2,1)S(1)}, u32[]{:S(2)}, u32[]{:S(2)}) async-start(bf16[12,256,128]{2,1,0:T(8,128)(2,1)} %bitcast.18), calls=%async_computation.1 | async-start | bytes 1572864 | tf_op jit(solution)/shard_map/sources/all_to_all | solution.py:103
  32.2 27.1 %all-to-all-done.1 = bf16[12,256,128]{2,1,0:T(8,128)(2,1)S(1)} async-done(((bf16[12,256,128]{2,1,0:T(8,128)(2,1)}), bf16[12,256,128]{2,1,0:T(8,128)(2,1)S(1)}, u32[]{:S(2)}, u32[]{:S(2)}) %all-to-all-start.1) | async-done | bytes 786464 | tf_op jit(solution)/shard_map/sources/all_to_all | solution.py:103
  59.3 0.0 copy-done.4
  59.3 0.0 copy-done.3
  59.3 0.0 copy-done
  59.3 1.3 aggregate_tiles.1
  60.6 8.9 %collective-permute-start = (bf16[32,128,128]{2,1,0:T(8,128)(2,1)S(1)}, bf16[32,128,128]{2,1,0:T(8,128)(2,1)S(1)}, u32[]{:S(2)}, u32[]{:S(2)}) collective-permute-start(bf16[32,128,128]{2,1,0:T(8,128)(2,1)S(1)} %get-tuple-element.7), channel_id=1, source_target_pairs={{0,12},{12,0},{1,13},{13,1},{2,14},{14,2},{3,15},{15,3},{4,16},{16... | collective-permute-start | bytes 3145736 | tf_op jit(solution)/shard_map/sum_core/ppermute | solution.py:128
  69.5 2.3 %collective-permute-done = bf16[32,128,128]{2,1,0:T(8,128)(2,1)S(1)} collective-permute-done((bf16[32,128,128]{2,1,0:T(8,128)(2,1)S(1)}, bf16[32,128,128]{2,1,0:T(8,128)(2,1)S(1)}, u32[]{:S(2)}, u32[]{:S(2)}) %collective-permute-start) | collective-permute-done | bytes 1048608 | tf_op jit(solution)/shard_map/sum_core/ppermute | solution.py:128
  71.8 0.3 add_convert_fusion
  72.1 0.0 copy-start.1
  72.1 0.0 copy-start.2
  72.1 20.8 %all_to_all.36 = bf16[8,512,128]{2,1,0:T(8,128)(2,1)S(1)} all-to-all(bf16[8,512,128]{2,1,0:T(8,128)(2,1)S(1)} %bitcast.17), channel_id=1, replica_groups=mesh['x'=4,'far'=4,'near'=2,'core'=2,'col'=12] {'x','near'}, dimensions={0} | all-to-all | bytes 2097152 | tf_op jit(solution)/shard_map/sum_x_near/all_to_all | solution.py:103
  92.9 0.1 add_convert_fusion.1
  93.1 13.0 %all_to_all.37.terms = bf16[4,128,128]{2,1,0:T(8,128)(2,1)S(1)} all-to-all(bf16[4,128,128]{2,1,0:T(8,128)(2,1)S(1)} %bitcast.19), channel_id=1, replica_groups=mesh['x'=4,'far'=4,'near'=2,'core'=2,'col'=12] {'far'}, dimensions={0} | all-to-all | bytes 262144 | tf_op jit(solution)/shard_map/sum_far/all_to_all | solution.py:103
  106.0 0.0 copy-done.1
  106.0 0.0 copy-done.2
  106.0 0.8 layer.1
  106.8 12.7 %all_to_all.38 = bf16[32,8,128]{2,1,0:T(8,128)(2,1)S(1)} all-to-all(bf16[32,8,128]{2,1,0:T(8,128)(2,1)S(1)} %bitcast.16), channel_id=1, replica_groups=mesh['x'=4,'far'=4,'near'=2,'core'=2,'col'=12] {'x','far','near'}, dimensions={0} | all-to-all | bytes 131072 | tf_op jit(solution)/shard_map/grad_xy/all_to_all | solution.py:103
  119.6 17.3 %all_to_all.39 = f32[24,8,128]{2,1,0:T(8,128)S(1)} all-to-all(f32[24,8,128]{2,1,0:T(8,128)S(1)} %broadcast_in_dim.10), channel_id=1, replica_groups=mesh['x'=4,'far'=4,'near'=2,'core'=2,'col'=12] {'core','col'}, dimensions={0} | all-to-all | bytes 196608 | tf_op jit(solution)/shard_map/grad_core_col/all_to_all | solution.py:103
  137.0 12.1 %all_to_all.40 = f32[32,8,128]{2,1,0:T(8,128)S(1)} all-to-all(f32[32,8,128]{2,1,0:T(8,128)S(1)} %broadcast_in_dim.11), channel_id=1, replica_groups=mesh['x'=4,'far'=4,'near'=2,'core'=2,'col'=12] {'x','far','near'}, dimensions={0} | all-to-all | bytes 262144 | tf_op jit(solution)/shard_map/grad_all/all_to_all | solution.py:103
  149.1 0.7 pad_maximum_fusion
  (5 shorter events, 0.1 us)
Async XLA Ops:
  0.6 58.7 %copy-start.4 = (s32[80]{0:T(128)S(1)}, s32[80]{0:T(128)}, u32[]{:S(2)}) copy-start(s32[80]{0:T(128)} %slot.1) | copy-start | bytes 964
  0.6 58.7 %copy-start.3 = (s32[80]{0:T(128)S(1)}, s32[80]{0:T(128)}, u32[]{:S(2)}) copy-start(s32[80]{0:T(128)} %dst.1) | copy-start | bytes 964
  0.7 58.7 %copy-start = (bf16[80,128,128]{2,1,0:T(8,128)(2,1)S(1)}, bf16[80,128,128]{2,1,0:T(8,128)(2,1)}, u32[]{:S(2)}) copy-start(bf16[80,128,128]{2,1,0:T(8,128)(2,1)} %tiles.1) | copy-start | bytes 7864324
  27.9 31.4 %all-to-all-start.1 = ((bf16[12,256,128]{2,1,0:T(8,128)(2,1)}), bf16[12,256,128]{2,1,0:T(8,128)(2,1)S(1)}, u32[]{:S(2)}, u32[]{:S(2)}) async-start(bf16[12,256,128]{2,1,0:T(8,128)(2,1)} %bitcast.18), calls=%async_computation.1 | async-start | bytes 1572864 | tf_op jit(solution)/shard_map/sources/all_to_all | solution.py:103
  60.6 11.2 %collective-permute-start = (bf16[32,128,128]{2,1,0:T(8,128)(2,1)S(1)}, bf16[32,128,128]{2,1,0:T(8,128)(2,1)S(1)}, u32[]{:S(2)}, u32[]{:S(2)}) collective-permute-start(bf16[32,128,128]{2,1,0:T(8,128)(2,1)S(1)} %get-tuple-element.7), channel_id=1, source_target_pairs={{0,12},{12,0},{1,13},{13,1},{2,14},{14,2},{3,15},{15,3},{4,16},{16... | collective-permute-start | bytes 3145736 | tf_op jit(solution)/shard_map/sum_core/ppermute | solution.py:128
  72.1 33.9 %copy-start.1 = (bf16[128,256]{1,0:T(8,128)(2,1)S(1)}, bf16[128,256]{1,0:T(8,128)(2,1)}, u32[]{:S(2)}) copy-start(bf16[128,256]{1,0:T(8,128)(2,1)} %weight.1) | copy-start | bytes 196612
  72.1 33.9 %copy-start.2 = (bf16[128,256]{1,0:T(8,128)(2,1)S(1)}, bf16[128,256]{1,0:T(8,128)(2,1)}, u32[]{:S(2)}) copy-start(bf16[128,256]{1,0:T(8,128)(2,1)} %cotangent.1) | copy-start | bytes 196612

commit v5 on v4

--- a/solution.py
+++ b/solution.py
@@ -99,8 +99,8 @@
     )(terms, weight, cotangent)
 
 
-def exchange(a, axis):
-    return lax.all_to_all(a, axis, 0, 0, tiled=True)
+def exchange(a, axis, groups=None):
+    return lax.all_to_all(a, axis, 0, 0, axis_index_groups=groups, tiled=True)
 
 
 def add_all(terms):
@@ -138,7 +138,7 @@
         part = add_all(exchange(grad.reshape(32, 8, 128), ("x", "far", "near")))
     with jax.named_scope("grad_core_col"):
         part = jnp.broadcast_to(part[None], (24, 8, 128))
-        part = jnp.sum(exchange(part, ("core", "col")), axis=0)
+        part = jnp.sum(exchange(part, ("core", "col"), [[12 * c + (z + 6) % 12 for c in (1, 0) for z in range(12)]]), axis=0)
     with jax.named_scope("grad_all"):
         whole = exchange(jnp.broadcast_to(part[None], (32, 8, 128)), ("x", "far", "near"))
         whole = whole.reshape(2, BLK, 128)

time: 151 us -> 149 us (0.987)
    all_to_all x6, blocking collectives: 100 us -> 98.8 us  [exchange(): return lax.all_to_all(a, axis, 0, 0, axis_index_groups=groups, tiled=True)]
where the time goes in v5:
time: 149 us
  blocking collectives  98.8 us (66%)
  waiting for transfers between devices  29.4 us (20%)
  starting transfers between devices  12.5 us (8%)
  Pallas kernels  4.32 us (3%)
  other arithmetic  2.04 us (1%)
    all_to_all x6, blocking collectives, exchange(): return lax.all_to_all(a, axis, 0, 0, axis_index_groups=groups, tiled=True)  98.8 us
    all_to_all x1, waiting for transfers between devices, exchange(): return lax.all_to_all(a, axis, 0, 0, axis_index_groups=groups, tiled=True)  27.1 us
    ppermute x1, starting transfers between devices, body(): other = lax.ppermute(theirs, 'core', [(0, 1), (1, 0)])  8.89 us
    all_to_all x1, starting transfers between devices, exchange(): return lax.all_to_all(a, axis, 0, 0, axis_index_groups=groups, tiled=True)  3.65 us
  transfers between devices with their start and end apart: 2, of which 2 were waited for; matrix products, arithmetic and copies ran while one was open for 0% of the time, Pallas kernels for 0%

profile of v5, /device:TPU:1, one launch (start us, length us, event | category | flops | bytes accessed | tf_op | source)
XLA Modules:
  0.0 148.6 jit_solution(13748039585528081009)
XLA Ops:
  0.6 0.0 copy-start.4
  0.6 0.0 copy-start.3
  0.7 0.0 copy-start
  0.7 0.9 add_bitcast_fusion.1
  1.5 0.1 broadcast_in_dim.8
  1.6 24.4 %all_to_all.35.asked = s32[12,1,128]{2,1,0:T(1,128)} all-to-all(s32[12,1,128]{2,1,0:T(1,128)S(1)} %broadcast_in_dim.8), channel_id=1, replica_groups=mesh['x'=4,'far'=4,'near'=2,'core'=2,'col'=12] {'col'}, dimensions={0} | all-to-all | bytes 12288 | tf_op jit(solution)/shard_map/ask/all_to_all | solution.py:103
  26.0 1.9 %pick_blocks.1 = bf16[12,2,128,128]{3,2,1,0:T(8,128)(2,1)} custom-call(s32[12,1,128]{2,1,0:T(1,128)} %all_to_all.35.asked, bf16[8,128,128]{2,1,0:T(8,128)(2,1)} %bitcast.20), custom_call_target="tpu_custom_call" | custom-call | tf_op jit(solution)/shard_map/pick/pick_blocks/pallas_call | solution.py:28
  27.9 3.6 %all-to-all-start.1 = ((bf16[12,256,128]{2,1,0:T(8,128)(2,1)}), bf16[12,256,128]{2,1,0:T(8,128)(2,1)S(1)}, u32[]{:S(2)}, u32[]{:S(2)}) async-start(bf16[12,256,128]{2,1,0:T(8,128)(2,1)} %bitcast.18), calls=%async_computation.1 | async-start | bytes 1572864 | tf_op jit(solution)/shard_map/sources/all_to_all | solution.py:103
  32.2 27.1 %all-to-all-done.1 = bf16[12,256,128]{2,1,0:T(8,128)(2,1)S(1)} async-done(((bf16[12,256,128]{2,1,0:T(8,128)(2,1)}), bf16[12,256,128]{2,1,0:T(8,128)(2,1)S(1)}, u32[]{:S(2)}, u32[]{:S(2)}) %all-to-all-start.1) | async-done | bytes 786464 | tf_op jit(solution)/shard_map/sources/all_to_all | solution.py:103
  59.3 0.0 copy-done.4
  59.3 0.0 copy-done.3
  59.3 0.0 copy-done
  59.3 1.6 %aggregate_tiles.1 = (f32[65,128,128]{2,1,0:T(8,128)S(1)}, bf16[32,128,128]{2,1,0:T(8,128)(2,1)S(1)}) custom-call(s32[80]{0:T(128)S(1)} %copy-done.3, s32[80]{0:T(128)S(1)} %copy-done.4, s32[1]{0:T(128)S(6)} %copy.10.count, s32[1]{0:T(128)} %bitcast.core, bf16[80,128,128]{2,1,0:T(8,128)(2,1)S(1)} %copy-done, bf16[24,128,128]{2,1,0:T(8,128)(2,1)S(1)} %bitcast.15), custom_call_target="tpu_custom_call" | custom-call | tf_op jit(solution)/shard_map/aggregate/aggregate_tiles/pallas_call | solution.py:60
  60.9 8.9 %collective-permute-start = (bf16[32,128,128]{2,1,0:T(8,128)(2,1)S(1)}, bf16[32,128,128]{2,1,0:T(8,128)(2,1)S(1)}, u32[]{:S(2)}, u32[]{:S(2)}) collective-permute-start(bf16[32,128,128]{2,1,0:T(8,128)(2,1)S(1)} %get-tuple-element.7), channel_id=1, source_target_pairs={{0,12},{12,0},{1,13},{13,1},{2,14},{14,2},{3,15},{15,3},{4,16},{16... | collective-permute-start | bytes 3145736 | tf_op jit(solution)/shard_map/sum_core/ppermute | solution.py:128
  69.8 2.3 %collective-permute-done = bf16[32,128,128]{2,1,0:T(8,128)(2,1)S(1)} collective-permute-done((bf16[32,128,128]{2,1,0:T(8,128)(2,1)S(1)}, bf16[32,128,128]{2,1,0:T(8,128)(2,1)S(1)}, u32[]{:S(2)}, u32[]{:S(2)}) %collective-permute-start) | collective-permute-done | bytes 1048608 | tf_op jit(solution)/shard_map/sum_core/ppermute | solution.py:128
  72.1 0.3 add_convert_fusion
  72.4 0.0 copy-start.1
  72.5 0.0 copy-start.2
  72.5 19.4 %all_to_all.36 = bf16[8,512,128]{2,1,0:T(8,128)(2,1)S(1)} all-to-all(bf16[8,512,128]{2,1,0:T(8,128)(2,1)S(1)} %bitcast.17), channel_id=1, replica_groups=mesh['x'=4,'far'=4,'near'=2,'core'=2,'col'=12] {'x','near'}, dimensions={0} | all-to-all | bytes 2097152 | tf_op jit(solution)/shard_map/sum_x_near/all_to_all | solution.py:103
  91.9 0.1 add_convert_fusion.1
  92.1 13.1 %all_to_all.37.terms = bf16[4,128,128]{2,1,0:T(8,128)(2,1)S(1)} all-to-all(bf16[4,128,128]{2,1,0:T(8,128)(2,1)S(1)} %bitcast.19), channel_id=1, replica_groups=mesh['x'=4,'far'=4,'near'=2,'core'=2,'col'=12] {'far'}, dimensions={0} | all-to-all | bytes 262144 | tf_op jit(solution)/shard_map/sum_far/all_to_all | solution.py:103
  105.1 0.0 copy-done.1
  105.1 0.0 copy-done.2
  105.1 0.8 layer.1
  105.9 12.7 %all_to_all.38 = bf16[32,8,128]{2,1,0:T(8,128)(2,1)S(1)} all-to-all(bf16[32,8,128]{2,1,0:T(8,128)(2,1)S(1)} %bitcast.16), channel_id=1, replica_groups=mesh['x'=4,'far'=4,'near'=2,'core'=2,'col'=12] {'x','far','near'}, dimensions={0} | all-to-all | bytes 131072 | tf_op jit(solution)/shard_map/grad_xy/all_to_all | solution.py:103
  118.7 17.0 %all_to_all.39 = f32[24,8,128]{2,1,0:T(8,128)S(1)} all-to-all(f32[24,8,128]{2,1,0:T(8,128)S(1)} %broadcast_in_dim.10), channel_id=1, replica_groups={{18,19,20,21,22,23,12,13,14,15,16,17,6,7,8,9,10,11,0,1,2,3,4,5},{42,43,..., dimensions={0} | all-to-all | bytes 196608 | tf_op jit(solution)/shard_map/grad_core_col/all_to_all | solution.py:103
  135.8 12.1 %all_to_all.40 = f32[32,8,128]{2,1,0:T(8,128)S(1)} all-to-all(f32[32,8,128]{2,1,0:T(8,128)S(1)} %broadcast_in_dim.11), channel_id=1, replica_groups=mesh['x'=4,'far'=4,'near'=2,'core'=2,'col'=12] {'x','far','near'}, dimensions={0} | all-to-all | bytes 262144 | tf_op jit(solution)/shard_map/grad_all/all_to_all | solution.py:103
  147.9 0.7 pad_maximum_fusion
  (5 shorter events, 0.1 us)
Async XLA Ops:
  0.6 58.7 %copy-start.4 = (s32[80]{0:T(128)S(1)}, s32[80]{0:T(128)}, u32[]{:S(2)}) copy-start(s32[80]{0:T(128)} %slot.1) | copy-start | bytes 964
  0.6 58.7 %copy-start.3 = (s32[80]{0:T(128)S(1)}, s32[80]{0:T(128)}, u32[]{:S(2)}) copy-start(s32[80]{0:T(128)} %dst.1) | copy-start | bytes 964
  0.7 58.7 %copy-start = (bf16[80,128,128]{2,1,0:T(8,128)(2,1)S(1)}, bf16[80,128,128]{2,1,0:T(8,128)(2,1)}, u32[]{:S(2)}) copy-start(bf16[80,128,128]{2,1,0:T(8,128)(2,1)} %tiles.1) | copy-start | bytes 7864324
  27.9 31.4 %all-to-all-start.1 = ((bf16[12,256,128]{2,1,0:T(8,128)(2,1)}), bf16[12,256,128]{2,1,0:T(8,128)(2,1)S(1)}, u32[]{:S(2)}, u32[]{:S(2)}) async-start(bf16[12,256,128]{2,1,0:T(8,128)(2,1)} %bitcast.18), calls=%async_computation.1 | async-start | bytes 1572864 | tf_op jit(solution)/shard_map/sources/all_to_all | solution.py:103
  60.9 11.2 %collective-permute-start = (bf16[32,128,128]{2,1,0:T(8,128)(2,1)S(1)}, bf16[32,128,128]{2,1,0:T(8,128)(2,1)S(1)}, u32[]{:S(2)}, u32[]{:S(2)}) collective-permute-start(bf16[32,128,128]{2,1,0:T(8,128)(2,1)S(1)} %get-tuple-element.7), channel_id=1, source_target_pairs={{0,12},{12,0},{1,13},{13,1},{2,14},{14,2},{3,15},{15,3},{4,16},{16... | collective-permute-start | bytes 3145736 | tf_op jit(solution)/shard_map/sum_core/ppermute | solution.py:128
  72.4 32.7 %copy-start.1 = (bf16[128,256]{1,0:T(8,128)(2,1)S(1)}, bf16[128,256]{1,0:T(8,128)(2,1)}, u32[]{:S(2)}) copy-start(bf16[128,256]{1,0:T(8,128)(2,1)} %weight.1) | copy-start | bytes 196612
  72.5 32.7 %copy-start.2 = (bf16[128,256]{1,0:T(8,128)(2,1)S(1)}, bf16[128,256]{1,0:T(8,128)(2,1)}, u32[]{:S(2)}) copy-start(bf16[128,256]{1,0:T(8,128)(2,1)} %cotangent.1) | copy-start | bytes 196612

commit v6 on v5

--- a/solution.py
+++ b/solution.py
@@ -7,6 +7,7 @@
 
 BLK = 128
 UNROLL = 20
+RING = [6 * (i % 2) + i // 2 for i in range(12)]
 AXES = ("x", "far", "near", "core", "col")
 SIZES = (4, 4, 2, 2, 12)
 
@@ -18,9 +19,9 @@
 
 def pick_kernel(asked, x_ref, out_ref):
     peers, listed = out_ref.shape[0], out_ref.shape[1]
-    for p in range(peers):
+    for i in range(peers):
         for k in range(listed):
-            out_ref[p, k] = x_ref[(asked[p, 0, 0] >> (8 * k)) & 255]
+            out_ref[i, k] = x_ref[(asked[RING[i], 0, 0] >> (8 * k)) & 255]
 
 
 def pick(asked, x_feat):
@@ -47,7 +48,10 @@
             xy = (d & 0x30) | ((d & 2) << 2) | ((d & 0xC) >> 1)
             place = ((d & 1) ^ me) * half + (xy >> 1)
             place = jnp.where(t < live, place, 2 * half)
-            acc[place] += jnp.dot(tiles[t], sources[slot[t]], preferred_element_type=F32)
+            p = slot[t] >> 1
+            place_in_ring = 2 * p - jnp.where(p >= 6, 11, 0)
+            source = sources[2 * place_in_ring + (slot[t] & 1)]
+            acc[place] += jnp.dot(tiles[t], source, preferred_element_type=F32)
         return carry
 
     lax.fori_loop(0, lax.div(live + (UNROLL - 1), UNROLL), group, 0)
@@ -119,7 +123,7 @@
     with jax.named_scope("pick"):
         picked = pick(asked, x_feat)
     with jax.named_scope("sources"):
-        sources = exchange(picked.reshape(cols, 2 * BLK, d_in), "col")
+        sources = exchange(picked.reshape(cols, 2 * BLK, d_in), "col", [RING])
         sources = sources.reshape(cols * 2, BLK, d_in)
     with jax.named_scope("aggregate"):
         core = lax.axis_index("core").astype(jnp.int32).reshape(1)

time: 149 us -> 147 us (0.987)
  starting transfers between devices: 12.5 us -> 7.83 us
  blocking collectives: 98.8 us -> 102 us
    ppermute x1, starting transfers between devices: 8.89 us -> 4.18 us  [body(): other = lax.ppermute(theirs, 'core', [(0, 1), (1, 0)])]
    all_to_all x6, blocking collectives: 98.8 us -> 102 us  [exchange(): return lax.all_to_all(a, axis, 0, 0, axis_index_groups=groups, tiled=True)]
where the time goes in v6:
time: 147 us; the launch traced here: 146 us
  blocking collectives  102 us (69%)
  waiting for transfers between devices  28.3 us (19%)
  starting transfers between devices  7.83 us (5%)
  Pallas kernels  5.05 us (3%)
  other arithmetic  2.04 us (1%)
    all_to_all x6, blocking collectives, exchange(): return lax.all_to_all(a, axis, 0, 0, axis_index_groups=groups, tiled=True)  102 us
    all_to_all x1, waiting for transfers between devices, exchange(): return lax.all_to_all(a, axis, 0, 0, axis_index_groups=groups, tiled=True)  26 us
    ppermute x1, starting transfers between devices, body(): other = lax.ppermute(theirs, 'core', [(0, 1), (1, 0)])  4.18 us
    all_to_all x1, starting transfers between devices, exchange(): return lax.all_to_all(a, axis, 0, 0, axis_index_groups=groups, tiled=True)  3.65 us
  transfers between devices with their start and end apart: 2, of which 2 were waited for; matrix products, arithmetic and copies ran while one was open for 0% of the time, Pallas kernels for 0%

profile of v6, /device:TPU:1, one launch (start us, length us, event | category | flops | bytes accessed | tf_op | source)
XLA Modules:
  0.0 146.3 jit_solution(8558748200546377345)
XLA Ops:
  0.6 0.0 copy-start.4
  0.6 0.0 copy-start.3
  0.7 0.0 copy-start
  0.7 0.9 add_bitcast_fusion.1
  1.5 0.1 broadcast_in_dim.8
  1.6 24.4 %all_to_all.35.asked = s32[12,1,128]{2,1,0:T(1,128)} all-to-all(s32[12,1,128]{2,1,0:T(1,128)S(1)} %broadcast_in_dim.8), channel_id=1, replica_groups=mesh['x'=4,'far'=4,'near'=2,'core'=2,'col'=12] {'col'}, dimensions={0} | all-to-all | bytes 12288 | tf_op jit(solution)/shard_map/ask/all_to_all | solution.py:107
  26.0 1.9 %pick_blocks.1 = bf16[12,2,128,128]{3,2,1,0:T(8,128)(2,1)} custom-call(s32[12,1,128]{2,1,0:T(1,128)} %all_to_all.35.asked, bf16[8,128,128]{2,1,0:T(8,128)(2,1)} %bitcast.20), custom_call_target="tpu_custom_call" | custom-call | tf_op jit(solution)/shard_map/pick/pick_blocks/pallas_call | solution.py:29
  27.9 3.6 %all-to-all-start.1 = ((bf16[12,256,128]{2,1,0:T(8,128)(2,1)}), bf16[12,256,128]{2,1,0:T(8,128)(2,1)S(1)}, u32[]{:S(2)}, u32[]{:S(2)}) async-start(bf16[12,256,128]{2,1,0:T(8,128)(2,1)} %bitcast.18), calls=%async_computation.1 | async-start | bytes 1572864 | tf_op jit(solution)/shard_map/sources/all_to_all | solution.py:107
  32.2 26.0 %all-to-all-done.1 = bf16[12,256,128]{2,1,0:T(8,128)(2,1)S(1)} async-done(((bf16[12,256,128]{2,1,0:T(8,128)(2,1)}), bf16[12,256,128]{2,1,0:T(8,128)(2,1)S(1)}, u32[]{:S(2)}, u32[]{:S(2)}) %all-to-all-start.1) | async-done | bytes 786464 | tf_op jit(solution)/shard_map/sources/all_to_all | solution.py:107
  58.2 0.0 copy-done.4
  58.2 0.0 copy-done.3
  58.2 0.0 copy-done
  58.2 2.3 %aggregate_tiles.1 = (f32[65,128,128]{2,1,0:T(8,128)S(1)}, bf16[32,128,128]{2,1,0:T(8,128)(2,1)S(1)}) custom-call(s32[80]{0:T(128)S(1)} %copy-done.3, s32[80]{0:T(128)S(1)} %copy-done.4, s32[1]{0:T(128)S(6)} %copy.10.count, s32[1]{0:T(128)} %bitcast.core, bf16[80,128,128]{2,1,0:T(8,128)(2,1)S(1)} %copy-done, bf16[24,128,128]{2,1,0:T(8,128)(2,1)S(1)} %bitcast.15), custom_call_target="tpu_custom_call" | custom-call | tf_op jit(solution)/shard_map/aggregate/aggregate_tiles/pallas_call | solution.py:64
  60.5 4.2 %collective-permute-start = (bf16[32,128,128]{2,1,0:T(8,128)(2,1)S(1)}, bf16[32,128,128]{2,1,0:T(8,128)(2,1)S(1)}, u32[]{:S(2)}, u32[]{:S(2)}) collective-permute-start(bf16[32,128,128]{2,1,0:T(8,128)(2,1)S(1)} %get-tuple-element.7), channel_id=1, source_target_pairs={{0,12},{12,0},{1,13},{13,1},{2,14},{14,2},{3,15},{15,3},{4,16},{16... | collective-permute-start | bytes 3145736 | tf_op jit(solution)/shard_map/sum_core/ppermute | solution.py:132
  64.7 2.3 %collective-permute-done = bf16[32,128,128]{2,1,0:T(8,128)(2,1)S(1)} collective-permute-done((bf16[32,128,128]{2,1,0:T(8,128)(2,1)S(1)}, bf16[32,128,128]{2,1,0:T(8,128)(2,1)S(1)}, u32[]{:S(2)}, u32[]{:S(2)}) %collective-permute-start) | collective-permute-done | bytes 1048608 | tf_op jit(solution)/shard_map/sum_core/ppermute | solution.py:132
  67.0 0.3 add_convert_fusion
  67.3 0.0 copy-start.1
  67.3 0.0 copy-start.2
  67.3 19.8 %all_to_all.36 = bf16[8,512,128]{2,1,0:T(8,128)(2,1)S(1)} all-to-all(bf16[8,512,128]{2,1,0:T(8,128)(2,1)S(1)} %bitcast.17), channel_id=1, replica_groups=mesh['x'=4,'far'=4,'near'=2,'core'=2,'col'=12] {'x','near'}, dimensions={0} | all-to-all | bytes 2097152 | tf_op jit(solution)/shard_map/sum_x_near/all_to_all | solution.py:107
  87.1 0.1 add_convert_fusion.1
  87.3 14.1 %all_to_all.37.terms = bf16[4,128,128]{2,1,0:T(8,128)(2,1)S(1)} all-to-all(bf16[4,128,128]{2,1,0:T(8,128)(2,1)S(1)} %bitcast.19), channel_id=1, replica_groups=mesh['x'=4,'far'=4,'near'=2,'core'=2,'col'=12] {'far'}, dimensions={0} | all-to-all | bytes 262144 | tf_op jit(solution)/shard_map/sum_far/all_to_all | solution.py:107
  101.4 0.0 copy-done.1
  101.4 0.0 copy-done.2
  101.4 0.8 layer.1
  102.2 12.7 %all_to_all.38 = bf16[32,8,128]{2,1,0:T(8,128)(2,1)S(1)} all-to-all(bf16[32,8,128]{2,1,0:T(8,128)(2,1)S(1)} %bitcast.16), channel_id=1, replica_groups=mesh['x'=4,'far'=4,'near'=2,'core'=2,'col'=12] {'x','far','near'}, dimensions={0} | all-to-all | bytes 131072 | tf_op jit(solution)/shard_map/grad_xy/all_to_all | solution.py:107
  115.0 18.5 %all_to_all.39 = f32[24,8,128]{2,1,0:T(8,128)S(1)} all-to-all(f32[24,8,128]{2,1,0:T(8,128)S(1)} %broadcast_in_dim.10), channel_id=1, replica_groups={{18,19,20,21,22,23,12,13,14,15,16,17,6,7,8,9,10,11,0,1,2,3,4,5},{42,43,..., dimensions={0} | all-to-all | bytes 196608 | tf_op jit(solution)/shard_map/grad_core_col/all_to_all | solution.py:107
  133.5 12.1 %all_to_all.40 = f32[32,8,128]{2,1,0:T(8,128)S(1)} all-to-all(f32[32,8,128]{2,1,0:T(8,128)S(1)} %broadcast_in_dim.11), channel_id=1, replica_groups=mesh['x'=4,'far'=4,'near'=2,'core'=2,'col'=12] {'x','far','near'}, dimensions={0} | all-to-all | bytes 262144 | tf_op jit(solution)/shard_map/grad_all/all_to_all | solution.py:107
  145.7 0.7 pad_maximum_fusion
  (5 shorter events, 0.1 us)
Async XLA Ops:
  0.6 57.5 %copy-start.4 = (s32[80]{0:T(128)S(1)}, s32[80]{0:T(128)}, u32[]{:S(2)}) copy-start(s32[80]{0:T(128)} %slot.1) | copy-start | bytes 964
  0.6 57.5 %copy-start.3 = (s32[80]{0:T(128)S(1)}, s32[80]{0:T(128)}, u32[]{:S(2)}) copy-start(s32[80]{0:T(128)} %dst.1) | copy-start | bytes 964
  0.7 57.5 %copy-start = (bf16[80,128,128]{2,1,0:T(8,128)(2,1)S(1)}, bf16[80,128,128]{2,1,0:T(8,128)(2,1)}, u32[]{:S(2)}) copy-start(bf16[80,128,128]{2,1,0:T(8,128)(2,1)} %tiles.1) | copy-start | bytes 7864324
  27.9 30.3 %all-to-all-start.1 = ((bf16[12,256,128]{2,1,0:T(8,128)(2,1)}), bf16[12,256,128]{2,1,0:T(8,128)(2,1)S(1)}, u32[]{:S(2)}, u32[]{:S(2)}) async-start(bf16[12,256,128]{2,1,0:T(8,128)(2,1)} %bitcast.18), calls=%async_computation.1 | async-start | bytes 1572864 | tf_op jit(solution)/shard_map/sources/all_to_all | solution.py:107
  60.5 6.5 %collective-permute-start = (bf16[32,128,128]{2,1,0:T(8,128)(2,1)S(1)}, bf16[32,128,128]{2,1,0:T(8,128)(2,1)S(1)}, u32[]{:S(2)}, u32[]{:S(2)}) collective-permute-start(bf16[32,128,128]{2,1,0:T(8,128)(2,1)S(1)} %get-tuple-element.7), channel_id=1, source_target_pairs={{0,12},{12,0},{1,13},{13,1},{2,14},{14,2},{3,15},{15,3},{4,16},{16... | collective-permute-start | bytes 3145736 | tf_op jit(solution)/shard_map/sum_core/ppermute | solution.py:132
  67.3 34.1 %copy-start.1 = (bf16[128,256]{1,0:T(8,128)(2,1)S(1)}, bf16[128,256]{1,0:T(8,128)(2,1)}, u32[]{:S(2)}) copy-start(bf16[128,256]{1,0:T(8,128)(2,1)} %weight.1) | copy-start | bytes 196612
  67.3 34.1 %copy-start.2 = (bf16[128,256]{1,0:T(8,128)(2,1)S(1)}, bf16[128,256]{1,0:T(8,128)(2,1)}, u32[]{:S(2)}) copy-start(bf16[128,256]{1,0:T(8,128)(2,1)} %cotangent.1) | copy-start | bytes 196612

commit v7 on v6

--- a/solution.py
+++ b/solution.py
@@ -6,8 +6,9 @@
 from jax.sharding import Mesh, PartitionSpec as P
 
 BLK = 128
-UNROLL = 20
+UNROLL = 40
 RING = [6 * (i % 2) + i // 2 for i in range(12)]
+NEAR = [4 * (i % 2) + i // 2 for i in range(8)]
 AXES = ("x", "far", "near", "core", "col")
 SIZES = (4, 4, 2, 2, 12)
 
@@ -45,8 +46,8 @@
         for u in range(UNROLL):
             t = g * UNROLL + u
             d = dst[t]
-            xy = (d & 0x30) | ((d & 2) << 2) | ((d & 0xC) >> 1)
-            place = ((d & 1) ^ me) * half + (xy >> 1)
+            inner = (d & 0x10) | ((d & 2) << 2) | ((d & 0x20) >> 3) | ((d & 0xC) >> 2)
+            place = ((d & 1) ^ me) * half + inner
             place = jnp.where(t < live, place, 2 * half)
             p = slot[t] >> 1
             place_in_ring = 2 * p - jnp.where(p >= 6, 11, 0)
@@ -132,7 +133,7 @@
         other = lax.ppermute(theirs, "core", [(0, 1), (1, 0)])
         summed = (mine[: other.shape[0]] + other.astype(F32)).astype(BF16)
     with jax.named_scope("sum_x_near"):
-        got = exchange(summed.reshape(xs * nears, fars * BLK, d_in), ("x", "near"))
+        got = exchange(summed.reshape(xs * nears, fars * BLK, d_in), ("x", "near"), [NEAR])
         summed = add_all(got).astype(BF16)
     with jax.named_scope("sum_far"):
         terms = exchange(summed.reshape(fars, BLK, d_in), "far")

time: 147 us -> 146 us (level)
  blocking collectives: 102 us -> 100 us
where the time goes in v7:
time: 146 us; the launch traced here: 145 us
  blocking collectives  100 us (68%)
  waiting for transfers between devices  28.3 us (19%)
  starting transfers between devices  8.89 us (6%)
  Pallas kernels  4.2 us (3%)
  other arithmetic  2.04 us (1%)
    all_to_all x6, blocking collectives, exchange(): return lax.all_to_all(a, axis, 0, 0, axis_index_groups=groups, tiled=True)  100 us
    all_to_all x1, waiting for transfers between devices, exchange(): return lax.all_to_all(a, axis, 0, 0, axis_index_groups=groups, tiled=True)  26 us
    ppermute x1, starting transfers between devices, body(): other = lax.ppermute(theirs, 'core', [(0, 1), (1, 0)])  5.24 us
    all_to_all x1, starting transfers between devices, exchange(): return lax.all_to_all(a, axis, 0, 0, axis_index_groups=groups, tiled=True)  3.65 us
  transfers between devices with their start and end apart: 2, of which 2 were waited for; matrix products, arithmetic and copies ran while one was open for 0% of the time, Pallas kernels for 0%

profile of v7, /device:TPU:1, one launch (start us, length us, event | category | flops | bytes accessed | tf_op | source)
XLA Modules:
  0.0 145.4 jit_solution(4987773529858696636)
XLA Ops:
  0.6 0.0 copy-start.4
  0.6 0.0 copy-start.3
  0.7 0.0 copy-start
  0.7 0.9 add_bitcast_fusion.1
  1.5 0.1 broadcast_in_dim.8
  1.6 24.4 %all_to_all.35.asked = s32[12,1,128]{2,1,0:T(1,128)} all-to-all(s32[12,1,128]{2,1,0:T(1,128)S(1)} %broadcast_in_dim.8), channel_id=1, replica_groups=mesh['x'=4,'far'=4,'near'=2,'core'=2,'col'=12] {'col'}, dimensions={0} | all-to-all | bytes 12288 | tf_op jit(solution)/shard_map/ask/all_to_all | solution.py:108
  26.0 1.9 %pick_blocks.1 = bf16[12,2,128,128]{3,2,1,0:T(8,128)(2,1)} custom-call(s32[12,1,128]{2,1,0:T(1,128)} %all_to_all.35.asked, bf16[8,128,128]{2,1,0:T(8,128)(2,1)} %bitcast.20), custom_call_target="tpu_custom_call" | custom-call | tf_op jit(solution)/shard_map/pick/pick_blocks/pallas_call | solution.py:30
  27.9 3.6 %all-to-all-start.1 = ((bf16[12,256,128]{2,1,0:T(8,128)(2,1)}), bf16[12,256,128]{2,1,0:T(8,128)(2,1)S(1)}, u32[]{:S(2)}, u32[]{:S(2)}) async-start(bf16[12,256,128]{2,1,0:T(8,128)(2,1)} %bitcast.18), calls=%async_computation.1 | async-start | bytes 1572864 | tf_op jit(solution)/shard_map/sources/all_to_all | solution.py:108
  32.2 26.0 %all-to-all-done.1 = bf16[12,256,128]{2,1,0:T(8,128)(2,1)S(1)} async-done(((bf16[12,256,128]{2,1,0:T(8,128)(2,1)}), bf16[12,256,128]{2,1,0:T(8,128)(2,1)S(1)}, u32[]{:S(2)}, u32[]{:S(2)}) %all-to-all-start.1) | async-done | bytes 786464 | tf_op jit(solution)/shard_map/sources/all_to_all | solution.py:108
  58.2 0.0 copy-done.4
  58.2 0.0 copy-done.3
  58.2 0.0 copy-done
  58.2 1.5 %aggregate_tiles.1 = (f32[65,128,128]{2,1,0:T(8,128)S(1)}, bf16[32,128,128]{2,1,0:T(8,128)(2,1)S(1)}) custom-call(s32[80]{0:T(128)S(1)} %copy-done.3, s32[80]{0:T(128)S(1)} %copy-done.4, s32[1]{0:T(128)S(6)} %copy.10.count, s32[1]{0:T(128)} %bitcast.core, bf16[80,128,128]{2,1,0:T(8,128)(2,1)S(1)} %copy-done, bf16[24,128,128]{2,1,0:T(8,128)(2,1)S(1)} %bitcast.15), custom_call_target="tpu_custom_call" | custom-call | tf_op jit(solution)/shard_map/aggregate/aggregate_tiles/pallas_call | solution.py:65
  59.7 5.2 %collective-permute-start = (bf16[32,128,128]{2,1,0:T(8,128)(2,1)S(1)}, bf16[32,128,128]{2,1,0:T(8,128)(2,1)S(1)}, u32[]{:S(2)}, u32[]{:S(2)}) collective-permute-start(bf16[32,128,128]{2,1,0:T(8,128)(2,1)S(1)} %get-tuple-element.7), channel_id=1, source_target_pairs={{0,12},{12,0},{1,13},{13,1},{2,14},{14,2},{3,15},{15,3},{4,16},{16... | collective-permute-start | bytes 3145736 | tf_op jit(solution)/shard_map/sum_core/ppermute | solution.py:133
  64.9 2.3 %collective-permute-done = bf16[32,128,128]{2,1,0:T(8,128)(2,1)S(1)} collective-permute-done((bf16[32,128,128]{2,1,0:T(8,128)(2,1)S(1)}, bf16[32,128,128]{2,1,0:T(8,128)(2,1)S(1)}, u32[]{:S(2)}, u32[]{:S(2)}) %collective-permute-start) | collective-permute-done | bytes 1048608 | tf_op jit(solution)/shard_map/sum_core/ppermute | solution.py:133
  67.2 0.3 add_convert_fusion
  67.5 0.0 copy-start.1
  67.5 0.0 copy-start.2
  67.5 19.8 %all_to_all.36 = bf16[8,512,128]{2,1,0:T(8,128)(2,1)S(1)} all-to-all(bf16[8,512,128]{2,1,0:T(8,128)(2,1)S(1)} %bitcast.17), channel_id=1, replica_groups={{0,384,24,408,192,576,216,600},{1,385,25,409,193,577,217,601},{2,386,26..., dimensions={0} | all-to-all | bytes 2097152 | tf_op jit(solution)/shard_map/sum_x_near/all_to_all | solution.py:108
  87.4 0.1 add_convert_fusion.1
  87.5 13.5 %all_to_all.37.terms = bf16[4,128,128]{2,1,0:T(8,128)(2,1)S(1)} all-to-all(bf16[4,128,128]{2,1,0:T(8,128)(2,1)S(1)} %bitcast.19), channel_id=1, replica_groups=mesh['x'=4,'far'=4,'near'=2,'core'=2,'col'=12] {'far'}, dimensions={0} | all-to-all | bytes 262144 | tf_op jit(solution)/shard_map/sum_far/all_to_all | solution.py:108
  101.0 0.0 copy-done.1
  101.0 0.0 copy-done.2
  101.0 0.8 layer.1
  101.9 12.6 %all_to_all.38 = bf16[32,8,128]{2,1,0:T(8,128)(2,1)S(1)} all-to-all(bf16[32,8,128]{2,1,0:T(8,128)(2,1)S(1)} %bitcast.16), channel_id=1, replica_groups=mesh['x'=4,'far'=4,'near'=2,'core'=2,'col'=12] {'x','far','near'}, dimensions={0} | all-to-all | bytes 131072 | tf_op jit(solution)/shard_map/grad_xy/all_to_all | solution.py:108
  114.5 18.1 %all_to_all.39 = f32[24,8,128]{2,1,0:T(8,128)S(1)} all-to-all(f32[24,8,128]{2,1,0:T(8,128)S(1)} %broadcast_in_dim.10), channel_id=1, replica_groups={{18,19,20,21,22,23,12,13,14,15,16,17,6,7,8,9,10,11,0,1,2,3,4,5},{42,43,..., dimensions={0} | all-to-all | bytes 196608 | tf_op jit(solution)/shard_map/grad_core_col/all_to_all | solution.py:108
  132.6 12.1 %all_to_all.40 = f32[32,8,128]{2,1,0:T(8,128)S(1)} all-to-all(f32[32,8,128]{2,1,0:T(8,128)S(1)} %broadcast_in_dim.11), channel_id=1, replica_groups=mesh['x'=4,'far'=4,'near'=2,'core'=2,'col'=12] {'x','far','near'}, dimensions={0} | all-to-all | bytes 262144 | tf_op jit(solution)/shard_map/grad_all/all_to_all | solution.py:108
  144.7 0.7 pad_maximum_fusion
  (5 shorter events, 0.1 us)
Async XLA Ops:
  0.6 57.5 %copy-start.4 = (s32[80]{0:T(128)S(1)}, s32[80]{0:T(128)}, u32[]{:S(2)}) copy-start(s32[80]{0:T(128)} %slot.1) | copy-start | bytes 964
  0.6 57.5 %copy-start.3 = (s32[80]{0:T(128)S(1)}, s32[80]{0:T(128)}, u32[]{:S(2)}) copy-start(s32[80]{0:T(128)} %dst.1) | copy-start | bytes 964
  0.7 57.5 %copy-start = (bf16[80,128,128]{2,1,0:T(8,128)(2,1)S(1)}, bf16[80,128,128]{2,1,0:T(8,128)(2,1)}, u32[]{:S(2)}) copy-start(bf16[80,128,128]{2,1,0:T(8,128)(2,1)} %tiles.1) | copy-start | bytes 7864324
  27.9 30.3 %all-to-all-start.1 = ((bf16[12,256,128]{2,1,0:T(8,128)(2,1)}), bf16[12,256,128]{2,1,0:T(8,128)(2,1)S(1)}, u32[]{:S(2)}, u32[]{:S(2)}) async-start(bf16[12,256,128]{2,1,0:T(8,128)(2,1)} %bitcast.18), calls=%async_computation.1 | async-start | bytes 1572864 | tf_op jit(solution)/shard_map/sources/all_to_all | solution.py:108
  59.7 7.5 %collective-permute-start = (bf16[32,128,128]{2,1,0:T(8,128)(2,1)S(1)}, bf16[32,128,128]{2,1,0:T(8,128)(2,1)S(1)}, u32[]{:S(2)}, u32[]{:S(2)}) collective-permute-start(bf16[32,128,128]{2,1,0:T(8,128)(2,1)S(1)} %get-tuple-element.7), channel_id=1, source_target_pairs={{0,12},{12,0},{1,13},{13,1},{2,14},{14,2},{3,15},{15,3},{4,16},{16... | collective-permute-start | bytes 3145736 | tf_op jit(solution)/shard_map/sum_core/ppermute | solution.py:133
  67.5 33.5 %copy-start.1 = (bf16[128,256]{1,0:T(8,128)(2,1)S(1)}, bf16[128,256]{1,0:T(8,128)(2,1)}, u32[]{:S(2)}) copy-start(bf16[128,256]{1,0:T(8,128)(2,1)} %weight.1) | copy-start | bytes 196612
  67.5 33.5 %copy-start.2 = (bf16[128,256]{1,0:T(8,128)(2,1)S(1)}, bf16[128,256]{1,0:T(8,128)(2,1)}, u32[]{:S(2)}) copy-start(bf16[128,256]{1,0:T(8,128)(2,1)} %cotangent.1) | copy-start | bytes 196612

commit v8 on v7

--- a/solution.py
+++ b/solution.py
@@ -18,22 +18,22 @@
 F32 = jnp.float32
 
 
-def pick_kernel(asked, x_ref, out_ref):
+def pick_kernel(asked, col, x_ref, out_ref):
     peers, listed = out_ref.shape[0], out_ref.shape[1]
     for i in range(peers):
         for k in range(listed):
-            out_ref[i, k] = x_ref[(asked[RING[i], 0, 0] >> (8 * k)) & 255]
+            out_ref[i, k] = x_ref[(asked[i, 0, col[0]] >> (8 * k)) & 255]
 
 
-def pick(asked, x_feat):
+def pick(asked, col, x_feat):
     peers, listed = SIZES[4], 2
     return pl.pallas_call(
         pick_kernel,
         out_shape=jax.ShapeDtypeStruct((peers, listed, BLK, x_feat.shape[1]), BF16),
-        in_specs=[SMEM, VMEM],
+        in_specs=[SMEM, SMEM, VMEM],
         out_specs=VMEM,
         name="pick_blocks",
-    )(asked, x_feat.reshape(-1, BLK, x_feat.shape[1]))
+    )(asked, col, x_feat.reshape(-1, BLK, x_feat.shape[1]))
 
 
 def aggregate_kernel(dst, slot, count, core, tiles, sources, acc, theirs):
@@ -120,9 +120,11 @@
     xs, fars, nears, cores, cols = SIZES
     with jax.named_scope("ask"):
         pair = src_blocks[:, 0] + 256 * src_blocks[:, 1]
-        asked = exchange(jnp.broadcast_to(pair[:, None, None], (cols, 1, 128)), "col")
+        pair = jnp.pad(pair, (0, 128 - cols))
+        asked = exchange(jnp.broadcast_to(pair[None, None], (cols, 1, 128)), "col", [RING])
     with jax.named_scope("pick"):
-        picked = pick(asked, x_feat)
+        col = lax.axis_index("col").astype(jnp.int32).reshape(1)
+        picked = pick(asked, col, x_feat)
     with jax.named_scope("sources"):
         sources = exchange(picked.reshape(cols, 2 * BLK, d_in), "col", [RING])
         sources = sources.reshape(cols * 2, BLK, d_in)

time: 146 us -> 148 us (1.014)
  blocking collectives: 100 us -> 76.3 us
  starting transfers between devices: 8.89 us -> 24.7 us
  waiting for transfers between devices: 28.3 us -> 37 us
    all_to_all x6 -> x5, blocking collectives: 100 us -> 76.3 us  [exchange(): return lax.all_to_all(a, axis, 0, 0, axis_index_groups=groups, tiled=True)]
    all_to_all x1 -> x2, starting transfers between devices: 3.65 us -> 19.4 us  [exchange(): return lax.all_to_all(a, axis, 0, 0, axis_index_groups=groups, tiled=True)]
    all_to_all x1 -> x2, waiting for transfers between devices: 26 us -> 34.7 us  [exchange(): return lax.all_to_all(a, axis, 0, 0, axis_index_groups=groups, tiled=True)]
  transfers between devices with their start and end apart: 2 -> 3, of which waited for: 2 -> 3; matrix products, arithmetic and copies ran while one was open for 0% -> 0% of each run, Pallas kernels for 0% -> 0%
where the time goes in v8:
time: 148 us; the launch traced here: 147 us
  blocking collectives  76.3 us (52%)
  waiting for transfers between devices  37 us (25%)
  starting transfers between devices  24.7 us (17%)
  Pallas kernels  4.21 us (3%)
  other arithmetic  2.04 us (1%)
    all_to_all x5, blocking collectives, exchange(): return lax.all_to_all(a, axis, 0, 0, axis_index_groups=groups, tiled=True)  76.3 us
    all_to_all x2, waiting for transfers between devices, exchange(): return lax.all_to_all(a, axis, 0, 0, axis_index_groups=groups, tiled=True)  34.7 us
    all_to_all x2, starting transfers between devices, exchange(): return lax.all_to_all(a, axis, 0, 0, axis_index_groups=groups, tiled=True)  19.4 us
    ppermute x1, starting transfers between devices, body(): other = lax.ppermute(theirs, 'core', [(0, 1), (1, 0)])  5.33 us
  transfers between devices with their start and end apart: 3, of which 3 were waited for; matrix products, arithmetic and copies ran while one was open for 0% of the time, Pallas kernels for 0%

profile of v8, /device:TPU:1, one launch (start us, length us, event | category | flops | bytes accessed | tf_op | source)
XLA Modules:
  0.0 146.9 jit_solution(10377362259639483307)
XLA Ops:
  0.6 0.0 copy-start.4
  0.6 0.0 copy-start.3
  0.7 0.0 copy-start
  0.7 0.9 add_bitcast_fusion.1
  1.5 0.6 broadcast_in_dim.8
  2.1 15.7 %all-to-all-start = ((s32[12,1,128]{2,1,0:T(1,128)}), s32[12,1,128]{2,1,0:T(1,128)S(1)}, u32[]{:S(2)}, u32[]{:S(2)}) async-start(s32[12,1,128]{2,1,0:T(1,128)} %broadcast_in_dim.8), calls=%async_computation | async-start | bytes 12288 | tf_op jit(solution)/shard_map/ask/all_to_all | solution.py:108
  17.8 8.8 %all-to-all-done.asked = s32[12,1,128]{2,1,0:T(1,128)S(1)} async-done(((s32[12,1,128]{2,1,0:T(1,128)}), s32[12,1,128]{2,1,0:T(1,128)S(1)}, u32[]{:S(2)}, u32[]{:S(2)}) %all-to-all-start) | async-done | bytes 6176 | tf_op jit(solution)/shard_map/ask/all_to_all | solution.py:108
  26.6 0.0 copy-start.5
  26.6 0.6 copy-done.5
  27.2 1.9 %pick_blocks.1 = bf16[12,2,128,128]{3,2,1,0:T(8,128)(2,1)} custom-call(s32[12,1,128]{2,1,0:T(1,128)} %copy-done.5, s32[1]{0:T(128)} %bitcast.2.col, bf16[8,128,128]{2,1,0:T(8,128)(2,1)} %bitcast.21), custom_call_target="tpu_custom_call" | custom-call | tf_op jit(solution)/shard_map/pick/pick_blocks/pallas_call | solution.py:30
  29.1 3.6 %all-to-all-start.1 = ((bf16[12,256,128]{2,1,0:T(8,128)(2,1)}), bf16[12,256,128]{2,1,0:T(8,128)(2,1)S(1)}, u32[]{:S(2)}, u32[]{:S(2)}) async-start(bf16[12,256,128]{2,1,0:T(8,128)(2,1)} %bitcast.19), calls=%async_computation.1 | async-start | bytes 1572864 | tf_op jit(solution)/shard_map/sources/all_to_all | solution.py:108
  33.4 25.9 %all-to-all-done.1 = bf16[12,256,128]{2,1,0:T(8,128)(2,1)S(1)} async-done(((bf16[12,256,128]{2,1,0:T(8,128)(2,1)}), bf16[12,256,128]{2,1,0:T(8,128)(2,1)S(1)}, u32[]{:S(2)}, u32[]{:S(2)}) %all-to-all-start.1) | async-done | bytes 786464 | tf_op jit(solution)/shard_map/sources/all_to_all | solution.py:108
  59.4 0.0 copy-done.4
  59.4 0.0 copy-done.3
  59.4 0.0 copy-done
  59.4 1.5 %aggregate_tiles.1 = (f32[65,128,128]{2,1,0:T(8,128)S(1)}, bf16[32,128,128]{2,1,0:T(8,128)(2,1)S(1)}) custom-call(s32[80]{0:T(128)S(1)} %copy-done.3, s32[80]{0:T(128)S(1)} %copy-done.4, s32[1]{0:T(128)S(6)} %copy.10.count, s32[1]{0:T(128)} %bitcast.core, bf16[80,128,128]{2,1,0:T(8,128)(2,1)S(1)} %copy-done, bf16[24,128,128]{2,1,0:T(8,128)(2,1)S(1)} %bitcast.16), custom_call_target="tpu_custom_call" | custom-call | tf_op jit(solution)/shard_map/aggregate/aggregate_tiles/pallas_call | solution.py:65
  60.9 5.3 %collective-permute-start = (bf16[32,128,128]{2,1,0:T(8,128)(2,1)S(1)}, bf16[32,128,128]{2,1,0:T(8,128)(2,1)S(1)}, u32[]{:S(2)}, u32[]{:S(2)}) collective-permute-start(bf16[32,128,128]{2,1,0:T(8,128)(2,1)S(1)} %get-tuple-element.7), channel_id=1, source_target_pairs={{0,12},{12,0},{1,13},{13,1},{2,14},{14,2},{3,15},{15,3},{4,16},{16... | collective-permute-start | bytes 3145736 | tf_op jit(solution)/shard_map/sum_core/ppermute | solution.py:135
  66.2 2.3 %collective-permute-done = bf16[32,128,128]{2,1,0:T(8,128)(2,1)S(1)} collective-permute-done((bf16[32,128,128]{2,1,0:T(8,128)(2,1)S(1)}, bf16[32,128,128]{2,1,0:T(8,128)(2,1)S(1)}, u32[]{:S(2)}, u32[]{:S(2)}) %collective-permute-start) | collective-permute-done | bytes 1048608 | tf_op jit(solution)/shard_map/sum_core/ppermute | solution.py:135
  68.5 0.3 add_convert_fusion
  68.8 0.0 copy-start.1
  68.8 0.0 copy-start.2
  68.8 19.8 %all_to_all.35 = bf16[8,512,128]{2,1,0:T(8,128)(2,1)S(1)} all-to-all(bf16[8,512,128]{2,1,0:T(8,128)(2,1)S(1)} %bitcast.18), channel_id=1, replica_groups={{0,384,24,408,192,576,216,600},{1,385,25,409,193,577,217,601},{2,386,26..., dimensions={0} | all-to-all | bytes 2097152 | tf_op jit(solution)/shard_map/sum_x_near/all_to_all | solution.py:108
  88.7 0.1 add_convert_fusion.1
  88.8 13.5 %all_to_all.36.terms = bf16[4,128,128]{2,1,0:T(8,128)(2,1)S(1)} all-to-all(bf16[4,128,128]{2,1,0:T(8,128)(2,1)S(1)} %bitcast.20), channel_id=1, replica_groups=mesh['x'=4,'far'=4,'near'=2,'core'=2,'col'=12] {'far'}, dimensions={0} | all-to-all | bytes 262144 | tf_op jit(solution)/shard_map/sum_far/all_to_all | solution.py:108
  102.3 0.0 copy-done.1
  102.3 0.0 copy-done.2
  102.3 0.8 layer.1
  103.1 12.6 %all_to_all.37 = bf16[32,8,128]{2,1,0:T(8,128)(2,1)S(1)} all-to-all(bf16[32,8,128]{2,1,0:T(8,128)(2,1)S(1)} %bitcast.17), channel_id=1, replica_groups=mesh['x'=4,'far'=4,'near'=2,'core'=2,'col'=12] {'x','far','near'}, dimensions={0} | all-to-all | bytes 131072 | tf_op jit(solution)/shard_map/grad_xy/all_to_all | solution.py:108
  115.8 18.2 %all_to_all.38 = f32[24,8,128]{2,1,0:T(8,128)S(1)} all-to-all(f32[24,8,128]{2,1,0:T(8,128)S(1)} %broadcast_in_dim.10), channel_id=1, replica_groups={{18,19,20,21,22,23,12,13,14,15,16,17,6,7,8,9,10,11,0,1,2,3,4,5},{42,43,..., dimensions={0} | all-to-all | bytes 196608 | tf_op jit(solution)/shard_map/grad_core_col/all_to_all | solution.py:108
  134.1 12.1 %all_to_all.39 = f32[32,8,128]{2,1,0:T(8,128)S(1)} all-to-all(f32[32,8,128]{2,1,0:T(8,128)S(1)} %broadcast_in_dim.11), channel_id=1, replica_groups=mesh['x'=4,'far'=4,'near'=2,'core'=2,'col'=12] {'x','far','near'}, dimensions={0} | all-to-all | bytes 262144 | tf_op jit(solution)/shard_map/grad_all/all_to_all | solution.py:108
  146.2 0.7 pad_maximum_fusion
  (6 shorter events, 0.1 us)
Async XLA Ops:
  0.6 58.7 %copy-start.4 = (s32[80]{0:T(128)S(1)}, s32[80]{0:T(128)}, u32[]{:S(2)}) copy-start(s32[80]{0:T(128)} %slot.1) | copy-start | bytes 964
  0.6 58.7 %copy-start.3 = (s32[80]{0:T(128)S(1)}, s32[80]{0:T(128)}, u32[]{:S(2)}) copy-start(s32[80]{0:T(128)} %dst.1) | copy-start | bytes 964
  0.7 58.7 %copy-start = (bf16[80,128,128]{2,1,0:T(8,128)(2,1)S(1)}, bf16[80,128,128]{2,1,0:T(8,128)(2,1)}, u32[]{:S(2)}) copy-start(bf16[80,128,128]{2,1,0:T(8,128)(2,1)} %tiles.1) | copy-start | bytes 7864324
  2.1 24.5 %all-to-all-start = ((s32[12,1,128]{2,1,0:T(1,128)}), s32[12,1,128]{2,1,0:T(1,128)S(1)}, u32[]{:S(2)}, u32[]{:S(2)}) async-start(s32[12,1,128]{2,1,0:T(1,128)} %broadcast_in_dim.8), calls=%async_computation | async-start | bytes 12288 | tf_op jit(solution)/shard_map/ask/all_to_all | solution.py:108
  26.6 0.6 copy-start.5
  29.1 30.2 %all-to-all-start.1 = ((bf16[12,256,128]{2,1,0:T(8,128)(2,1)}), bf16[12,256,128]{2,1,0:T(8,128)(2,1)S(1)}, u32[]{:S(2)}, u32[]{:S(2)}) async-start(bf16[12,256,128]{2,1,0:T(8,128)(2,1)} %bitcast.19), calls=%async_computation.1 | async-start | bytes 1572864 | tf_op jit(solution)/shard_map/sources/all_to_all | solution.py:108
  60.9 7.6 %collective-permute-start = (bf16[32,128,128]{2,1,0:T(8,128)(2,1)S(1)}, bf16[32,128,128]{2,1,0:T(8,128)(2,1)S(1)}, u32[]{:S(2)}, u32[]{:S(2)}) collective-permute-start(bf16[32,128,128]{2,1,0:T(8,128)(2,1)S(1)} %get-tuple-element.7), channel_id=1, source_target_pairs={{0,12},{12,0},{1,13},{13,1},{2,14},{14,2},{3,15},{15,3},{4,16},{16... | collective-permute-start | bytes 3145736 | tf_op jit(solution)/shard_map/sum_core/ppermute | solution.py:135
  68.8 33.5 %copy-start.1 = (bf16[128,256]{1,0:T(8,128)(2,1)S(1)}, bf16[128,256]{1,0:T(8,128)(2,1)}, u32[]{:S(2)}) copy-start(bf16[128,256]{1,0:T(8,128)(2,1)} %weight.1) | copy-start | bytes 196612
  68.8 33.5 %copy-start.2 = (bf16[128,256]{1,0:T(8,128)(2,1)S(1)}, bf16[128,256]{1,0:T(8,128)(2,1)}, u32[]{:S(2)}) copy-start(bf16[128,256]{1,0:T(8,128)(2,1)} %cotangent.1) | copy-start | bytes 196612
